TPU v7x, 512 devices: a whole 4x4x16 slice. The times are simulated.
512 devices in a mesh: bank: 128 (over y, z, core), head: 4 (over x).
Axes of the slice: x: 4, y: 4, z: 16, core: 2. Of those that a mesh axis runs over, the one named last changes fastest.
Arguments:
- inputs: bfloat16 [4096, 768], P('bank'), may hold values from -6 to 6
- positives: bfloat16 [4096, 768], P('bank'), may hold values from -0.21875 to 0.21875
- margins: float32 [4096, 32], P('bank'), may hold values from -6 to 6
- neg_block: int32 [4096, 32], P('bank'), may hold values from 0 to 511, as said below
- neg_row: int32 [4096, 32], P('bank'), may hold values from 0 to 127
- block_home: int32 [512], replicated, may hold values from 0 to 511, as said below
- bank: bfloat16 [65536, 768], P('bank'), may hold values from -0.21875 to 0.21875
- up_weight: bfloat16 [768, 3072], P(None, 'head'), may hold values from -0.21875 to 0.21875
- up_bias: float32 [3072], P('head'), may hold values from -5 to 5
- down_weight: bfloat16 [3072, 768], P('head'), may hold values from -0.109375 to 0.109375
Outputs:
- grad_inputs: bfloat16 [4096, 768], P(('bank', 'head'))
- grad_down: bfloat16 [3072, 768], P('head')
Inputs may be any that keep to these rules, and one draw needn't show every extreme that they name: `block_home`: storage position p holds block rows p * 128 to p * 128 + 127 of bank; each position holds one block. `neg_block`: call p // 4, with p the storage position of a negative's block, its owner. Among the 256 pairs of an aligned group of 8 queries, at most 4 have one owner; in every group some owners have exactly 4, and one owner has exactly 4 in every group.
All inputs are finite; a program needn't handle non-finite values.
Results may differ from a plain program's by a relative error of at most 0.02.
Values may be sent and summed in bfloat16 or wider, within the bound.
A program may use at most 64 MiB of HBM per device.

v0:
```python
import math

import jax
import jax.numpy as jnp
from jax import lax
from jax.sharding import PartitionSpec as P

NEG = 32
BLOCK_ROWS = 128


def gelu_tanh(values):
    return jax.nn.gelu(values, approximate=True)


def on_device(
    inputs,
    positives,
    margins,
    neg_block,
    neg_row,
    block_home,
    bank,
    up_weight,
    up_bias,
    down_weight,
):
    head_count = lax.axis_size("head")
    bank_count = lax.axis_size("bank")
    head_index = lax.axis_index("head")
    width = inputs.shape[1]
    quarter = inputs.shape[0] // head_count
    pre = jnp.dot(inputs, up_weight, preferred_element_type=jnp.float32) + up_bias
    hidden = gelu_tanh(pre).astype(jnp.bfloat16)
    partial_emb = jnp.dot(hidden, down_weight, preferred_element_type=jnp.float32)
    own_inputs = lax.dynamic_slice_in_dim(inputs, head_index * quarter, quarter, 0)
    own_positives = lax.dynamic_slice_in_dim(positives, head_index * quarter, quarter, 0)
    own_margins = lax.dynamic_slice_in_dim(margins, head_index * quarter, quarter, 0)
    own_blocks = lax.dynamic_slice_in_dim(neg_block, head_index * quarter, quarter, 0)
    own_rows = lax.dynamic_slice_in_dim(neg_row, head_index * quarter, quarter, 0)
    total = lax.psum(partial_emb.astype(jnp.bfloat16), "head").astype(jnp.float32)
    branch = lax.dynamic_slice_in_dim(total, head_index * quarter, quarter, 0)
    query_emb = own_inputs.astype(jnp.float32) + branch
    embedded = query_emb.astype(jnp.bfloat16)
    positive_score = jnp.sum(
        embedded.astype(jnp.float32) * own_positives.astype(jnp.float32), axis=1
    )
    offsets = (positive_score[:, None] - own_margins).astype(jnp.bfloat16)
    per_owner = bank.shape[0] // BLOCK_ROWS
    position = block_home[own_blocks]
    owners = (position // per_owner).reshape(-1)
    local_row = (position % per_owner * BLOCK_ROWS + own_rows).reshape(-1)
    offsets_flat = offsets.reshape(-1)
    pair_count = owners.shape[0]
    capacity = 2 * pair_count // bank_count
    columns = jnp.arange(bank_count, dtype=jnp.int32)
    onehot = (owners[:, None] == columns[None, :]).astype(jnp.int32)
    rank_in = jnp.sum(onehot * jnp.cumsum(onehot, axis=0), axis=1) - 1
    slot_ids = owners * capacity + rank_in
    pair_of_slot = (
        jnp.full((bank_count * capacity,), pair_count, jnp.int32)
        .at[slot_ids]
        .set(jnp.arange(pair_count, dtype=jnp.int32))
    )
    filled = pair_of_slot < pair_count
    pair_safe = jnp.minimum(pair_of_slot, pair_count - 1)
    query_slot = pair_safe // NEG
    sent_emb = jnp.where(filled[:, None], embedded[query_slot], jnp.zeros((), jnp.bfloat16))
    sent_offsets = jnp.where(filled, offsets_flat[pair_safe], jnp.zeros((), jnp.bfloat16))
    sent_rows = jnp.where(filled, local_row[pair_safe], 0)
    grid_shape = (bank_count, capacity)
    emb_part = lax.all_to_all(
        sent_emb.reshape(bank_count, capacity, width),
        "bank",
        split_axis=0,
        concat_axis=0,
        tiled=True,
    )
    row_part = lax.all_to_all(
        sent_rows.reshape(grid_shape), "bank", split_axis=0, concat_axis=0, tiled=True
    )
    offset_part = lax.all_to_all(
        sent_offsets.reshape(grid_shape), "bank", split_axis=0, concat_axis=0, tiled=True
    )
    neighbours = bank[row_part]
    scores = jnp.einsum("scd,scd->sc", emb_part, neighbours, preferred_element_type=jnp.float32)
    residual = offset_part.astype(jnp.float32) - scores
    weighted_part = (residual[:, :, None] * neighbours).astype(jnp.bfloat16)
    weighted = lax.all_to_all(weighted_part, "bank", split_axis=0, concat_axis=0, tiled=True)
    rounded = lax.all_to_all(
        residual.astype(jnp.bfloat16), "bank", split_axis=0, concat_axis=0, tiled=True
    )
    weighted = weighted.reshape(-1, width)
    rounded = rounded.reshape(-1)
    query_ids = jnp.arange(quarter, dtype=jnp.int32)
    selector = (filled[None, :] & (query_slot[None, :] == query_ids[:, None])).astype(jnp.bfloat16)
    weighted_sum = jnp.dot(selector, weighted, preferred_element_type=jnp.float32)
    residual_sum = jnp.sum(
        selector.astype(jnp.float32) * rounded.astype(jnp.float32)[None, :], axis=1
    )
    gradient = 2.0 * own_positives.astype(jnp.float32) * residual_sum[:, None] - 2.0 * weighted_sum
    grad_rounded = gradient.astype(jnp.bfloat16)
    grad_all = lax.all_gather(grad_rounded, "head", axis=0, tiled=True)
    hidden_grad = lax.dot_general(
        grad_all, down_weight, (((1,), (1,)), ((), ())), preferred_element_type=jnp.float32
    )
    unused, pullback = jax.vjp(gelu_tanh, pre)
    pre_grad = pullback(hidden_grad)[0].astype(jnp.bfloat16)
    carried = lax.psum_scatter(
        lax.dot_general(
            pre_grad, up_weight, (((1,), (1,)), ((), ())), preferred_element_type=jnp.float32
        ).astype(jnp.bfloat16),
        "head",
        scatter_dimension=0,
        tiled=True,
    ).astype(jnp.float32)
    grad_inputs = (gradient + carried).astype(jnp.bfloat16)
    local_down = lax.dot_general(
        hidden, grad_all, (((0,), (0,)), ((), ())), preferred_element_type=jnp.float32
    )
    summed = lax.psum(local_down, "bank")
    queries_all = inputs.shape[0] * bank_count
    grad_down = (summed / math.sqrt(queries_all)).astype(jnp.bfloat16)
    return (grad_inputs, grad_down)


def solution(mesh):
    return jax.shard_map(
        on_device,
        mesh=mesh,
        in_specs=(
            P("bank", None),
            P("bank", None),
            P("bank", None),
            P("bank", None),
            P("bank", None),
            P(),
            P("bank", None),
            P(None, "head"),
            P("head"),
            P("head", None),
        ),
        out_specs=(P(("bank", "head"), None), P("head", None)),
        check_vma=False,
    )
```

profile of v0, /device:TPU:1, one launch (start us, length us, event | category | flops | bytes accessed | tf_op | source)
XLA Modules:
  0.0 595.2 jit_solution(14880874449246726593)
XLA Ops:
  8.0 0.8 compare_select_fusion.1
  8.9 1.9 gather_fusion
  11.6 1.4 scatter_custom_fusion
  13.7 14.6 %psum.14 = bf16[32,768]{1,0:T(8,128)(2,1)S(1)} all-reduce(bf16[32,768]{1,0:T(8,128)(2,1)S(1)} %convolution_convert_fusion.1), channel_id=1, replica_groups=mesh['bank'=128,'head'=4] {'head'}, use_global_device_ids=true, to_apply=%region_4.5 | all-reduce | flops 24576 | bytes 98304 | tf_op jit(solution)/shard_map/psum | solution.py:41
  29.3 3.4 gather_fusion.1
  33.4 23.3 %all-to-all-start = ((bf16[128,1,4]{2,1,0:T(2,128)(2,1)}), bf16[128,1,4]{2,1,0:T(2,128)(2,1)S(1)}, u32[]{:S(2)}, u32[]{:S(2)}) async-start(bf16[128,1,4]{2,1,0:T(2,128)(2,1)} %all_to_all.35), calls=%async_computation | async-start | bytes 131072 | tf_op jit(solution)/shard_map/all_to_all | solution.py:82
  57.6 3.5 gather_fusion.3
  62.0 2.7 gather_fusion.2
  64.7 1.7 gather.29
  66.4 5.4 all-to-all-done
  71.8 10.8 %all-to-all-start.2 = ((s32[128,1,4]{2,1,0:T(1,128)}), s32[128,1,4]{2,1,0:T(1,128)S(1)}, u32[]{:S(2)}, u32[]{:S(2)}) async-start(s32[128,1,4]{2,1,0:T(1,128)} %bitcast.8), calls=%async_computation.2 | async-start | bytes 131072 | tf_op jit(solution)/shard_map/all_to_all | solution.py:79
  82.6 1.3 broadcast_select_fusion
  83.9 13.5 %all-to-all-done.2 = s32[128,1,4]{2,1,0:T(1,128)S(1)} async-done(((s32[128,1,4]{2,1,0:T(1,128)}), s32[128,1,4]{2,1,0:T(1,128)S(1)}, u32[]{:S(2)}, u32[]{:S(2)}) %all-to-all-start.2) | async-done | bytes 2080 | tf_op jit(solution)/shard_map/all_to_all | solution.py:79
  97.5 7.8 %all-to-all-start.1 = ((bf16[128,4,768]{2,1,0:T(4,128)(2,1)}), bf16[128,4,768]{2,1,0:T(4,128)(2,1)}, u32[]{:S(2)}, u32[]{:S(2)}) async-start(bf16[128,4,768]{2,1,0:T(4,128)(2,1)} %broadcast_select_fusion), calls=%async_computation.1 | async-start | bytes 1572864 | tf_op jit(solution)/shard_map/all_to_all | solution.py:72
  105.5 2.7 gather_fusion.4
  108.2 1.7 reshape.240
  109.9 38.7 %all-to-all-done.1 = bf16[128,4,768]{2,1,0:T(4,128)(2,1)} async-done(((bf16[128,4,768]{2,1,0:T(4,128)(2,1)}), bf16[128,4,768]{2,1,0:T(4,128)(2,1)}, u32[]{:S(2)}, u32[]{:S(2)}) %all-to-all-start.1) | async-done | bytes 786464 | tf_op jit(solution)/shard_map/all_to_all | solution.py:72
  148.5 1.7 fusion
  150.9 8.1 %all-to-all-start.3 = ((bf16[128,1,4]{2,1,0:T(2,128)(2,1)}), bf16[128,1,4]{2,1,0:T(2,128)(2,1)S(1)}, u32[]{:S(2)}, u32[]{:S(2)}) async-start(bf16[128,1,4]{2,1,0:T(2,128)(2,1)} %copy.23), calls=%async_computation.3 | async-start | bytes 131072 | tf_op jit(solution)/shard_map/all_to_all | solution.py:90
  159.0 1.3 fusion.1
  160.3 13.7 %all-to-all-done.3 = bf16[128,1,4]{2,1,0:T(2,128)(2,1)S(1)} async-done(((bf16[128,1,4]{2,1,0:T(2,128)(2,1)}), bf16[128,1,4]{2,1,0:T(2,128)(2,1)S(1)}, u32[]{:S(2)}, u32[]{:S(2)}) %all-to-all-start.3) | async-done | bytes 1056 | tf_op jit(solution)/shard_map/all_to_all | solution.py:90
  174.0 6.6 %all-to-all-start.4 = ((bf16[128,4,768]{2,1,0:T(4,128)(2,1)}), bf16[128,4,768]{2,1,0:T(4,128)(2,1)S(1)}, u32[]{:S(2)}, u32[]{:S(2)}) async-start(bf16[128,4,768]{2,1,0:T(4,128)(2,1)} %fusion.1), calls=%async_computation.4 | async-start | bytes 1572864 | tf_op jit(solution)/shard_map/all_to_all | solution.py:89
  181.1 43.1 %all-to-all-done.4 = bf16[128,4,768]{2,1,0:T(4,128)(2,1)S(1)} async-done(((bf16[128,4,768]{2,1,0:T(4,128)(2,1)}), bf16[128,4,768]{2,1,0:T(4,128)(2,1)S(1)}, u32[]{:S(2)}, u32[]{:S(2)}) %all-to-all-start.4) | async-done | bytes 786464 | tf_op jit(solution)/shard_map/all_to_all | solution.py:89
  224.3 1.1 reshape.204
  225.3 1.3 fusion.41
  226.7 9.0 %all_gather.3 = bf16[32,768]{1,0:T(8,128)(2,1)S(1)} all-gather(bf16[8,768]{1,0:T(8,128)(2,1)S(1)} %get-tuple-element.11), channel_id=1, replica_groups=mesh['bank'=128,'head'=4] {'head'}, dimensions={0}, use_global_device_ids=true | all-gather | bytes 61440 | tf_op jit(solution)/shard_map/all_gather | solution.py:103
  235.7 1.5 convolution_convert_fusion
  237.3 1.9 fusion.40
  239.2 18.0 %reduce-scatter.2.cloned.1.call-done = bf16[8,768]{1,0:T(8,128)(2,1)} async-done(((bf16[32,768]{1,0:T(8,128)(2,1)}), bf16[8,768]{1,0:T(8,128)(2,1)}) %reduce-scatter.2.cloned.1.call-update) | async-done | bytes 12304 | tf_op jit(solution)/shard_map/reduce_scatter | solution.py:109
  257.2 1.3 add_convert_fusion
  258.5 326.4 %all-reduce.2.cloned.1.call-done = f32[768,768]{1,0:T(8,128)} async-done(((f32[768,768]{1,0:T(8,128)}), f32[768,768]{1,0:T(8,128)}) %all-reduce.2.cloned.1.call-update) | async-done | bytes 2359312 | tf_op jit(solution)/shard_map/psum | solution.py:121
  584.9 2.9 multiply_convert_fusion
  (60 shorter events, 6.3 us)
Async XLA Ops:
  8.0 5.4 copy-start
  8.0 0.9 copy-start.1
  8.9 4.1 copy-start.3
  8.9 4.1 copy-start.4
  8.9 4.1 copy-start.6
  13.0 15.3 %copy-start.5 = (bf16[32,768]{1,0:T(8,128)(2,1)S(1)}, bf16[32,768]{1,0:T(8,128)(2,1)}, u32[]{:S(2)}) copy-start(bf16[32,768]{1,0:T(8,128)(2,1)} %param.11) | copy-start | bytes 147460
  33.4 38.3 %all-to-all-start = ((bf16[128,1,4]{2,1,0:T(2,128)(2,1)}), bf16[128,1,4]{2,1,0:T(2,128)(2,1)S(1)}, u32[]{:S(2)}, u32[]{:S(2)}) async-start(bf16[128,1,4]{2,1,0:T(2,128)(2,1)} %all_to_all.35), calls=%async_computation | async-start | bytes 131072 | tf_op jit(solution)/shard_map/all_to_all | solution.py:82
  71.8 25.7 %all-to-all-start.2 = ((s32[128,1,4]{2,1,0:T(1,128)}), s32[128,1,4]{2,1,0:T(1,128)S(1)}, u32[]{:S(2)}, u32[]{:S(2)}) async-start(s32[128,1,4]{2,1,0:T(1,128)} %bitcast.8), calls=%async_computation.2 | async-start | bytes 131072 | tf_op jit(solution)/shard_map/all_to_all | solution.py:79
  83.9 21.5 %copy-start.2 = (bf16[512,768]{1,0:T(8,128)(2,1)S(1)}, bf16[512,768]{1,0:T(8,128)(2,1)}, u32[]{:S(2)}) copy-start(bf16[512,768]{1,0:T(8,128)(2,1)} %param.16) | copy-start | bytes 2359300
  97.5 51.1 %all-to-all-start.1 = ((bf16[128,4,768]{2,1,0:T(4,128)(2,1)}), bf16[128,4,768]{2,1,0:T(4,128)(2,1)}, u32[]{:S(2)}, u32[]{:S(2)}) async-start(bf16[128,4,768]{2,1,0:T(4,128)(2,1)} %broadcast_select_fusion), calls=%async_computation.1 | async-start | bytes 1572864 | tf_op jit(solution)/shard_map/all_to_all | solution.py:72
  150.9 23.1 %all-to-all-start.3 = ((bf16[128,1,4]{2,1,0:T(2,128)(2,1)}), bf16[128,1,4]{2,1,0:T(2,128)(2,1)S(1)}, u32[]{:S(2)}, u32[]{:S(2)}) async-start(bf16[128,1,4]{2,1,0:T(2,128)(2,1)} %copy.23), calls=%async_computation.3 | async-start | bytes 131072 | tf_op jit(solution)/shard_map/all_to_all | solution.py:90
  174.0 50.3 %all-to-all-start.4 = ((bf16[128,4,768]{2,1,0:T(4,128)(2,1)}), bf16[128,4,768]{2,1,0:T(4,128)(2,1)S(1)}, u32[]{:S(2)}, u32[]{:S(2)}) async-start(bf16[128,4,768]{2,1,0:T(4,128)(2,1)} %fusion.1), calls=%async_computation.4 | async-start | bytes 1572864 | tf_op jit(solution)/shard_map/all_to_all | solution.py:89
  180.7 76.5 %reduce-scatter.2.cloned.1.call-start = ((), (), s32[]{:S(2)}) async-start(), calls=%async_computation.6 | async-start | bytes 61440 | tf_op jit(solution)/shard_map/reduce_scatter | solution.py:109
  237.2 347.7 %all-reduce.2.cloned.1.call-start = ((), (), s32[]{:S(2)}) async-start(), calls=%async_computation.7 | async-start | bytes 4718592 | tf_op jit(solution)/shard_map/psum | solution.py:121
Sparse Core Ops, SparseCore 0:
  237.3 19.8 reduce-scatter.1
Sparse Core Ops, SparseCore 1:
  241.5 343.4 all-reduce.1
where the time goes:
time: 596 us; the launch traced here: 595 us
  waiting for transfers between devices  459 us (77%)
  starting transfers between devices  56.7 us (10%)
  blocking collectives  23.6 us (4%)
  local copies, waits for them, and re-layouts  23 us (4%)
  between operations  15.8 us (3%)
  other arithmetic  11.8 us (2%)
    psum x1, waiting for transfers between devices, on_device(): summed = lax.psum(local_down, 'bank')  326 us
    all_to_all x1, waiting for transfers between devices, on_device(): lax.all_to_all(weighted_part, 'bank', split_axis=0, concat_axis=0, tiled=...  43.1 us
    all_to_all x1, waiting for transfers between devices, on_device(): lax.all_to_all(sent_emb.reshape(bank_count, capacity, width), 'bank', spl...  38.7 us
    all_to_all x1, starting transfers between devices, on_device(): lax.all_to_all(sent_offsets.reshape(grid_shape), 'bank', split_axis=0, co...  23.3 us
    reduce_scatter x1, waiting for transfers between devices, on_device(): lax.psum_scatter(lax.dot_general(pre_grad, up_weight, (((1,), (1,)), ((),...  18 us
    psum x1, blocking collectives, on_device(): lax.psum(partial_emb.astype(jnp.bfloat16), 'head').astype(jnp.float32)  14.6 us
    all_to_all x1, waiting for transfers between devices, on_device(): lax.all_to_all(residual.astype(jnp.bfloat16), 'bank', split_axis=0, conca...  13.7 us
    all_to_all x1, waiting for transfers between devices, on_device(): lax.all_to_all(sent_rows.reshape(grid_shape), 'bank', split_axis=0, conca...  13.5 us
  transfers between devices with their start and end apart: 7, of which 7 were waited for; matrix products, arithmetic and copies ran while one was open for 3% of the time, Pallas kernels for 0%

commit v1 on v0

v1 whole, which is shorter than its diff:
```python
import functools
import math

import jax
import jax.numpy as jnp
from jax import lax
from jax.experimental import pallas as pl
from jax.experimental.pallas import tpu as pltpu
from jax.sharding import PartitionSpec as P

MESH = pl.DeviceIdType.MESH
F32 = jnp.float32
BF16 = jnp.bfloat16
I32 = jnp.int32
NEG = 32
BLOCK_ROWS = 128
QH = 8
PAIRS = QH * NEG
K0 = math.sqrt(2.0 / math.pi)
K1 = 0.044715


def iota(shape, axis):
    return lax.broadcasted_iota(I32, shape, axis)


def dot(a, b, ca=1, cb=0):
    return lax.dot_general(a, b, (((ca,), (cb,)), ((), ())), preferred_element_type=F32)


def fold(rows):
    w = rows.shape[1] // 2
    return jnp.concatenate([rows[:, :w], rows[:, w:]], axis=0)


def unfold(rows):
    return jnp.concatenate([rows[:QH], rows[QH:]], axis=1)


def kernel(
    dims,
    in_ref, pos_ref, nb_ref, nr_ref, mg_ref, home_ref, bank_ref, up_ref, bias_ref, down_ref,
    gi_ref, gd_ref,
    meta_all, e_all, ps_all, h_all, f_all, gd_all,
    xs, xr, xs2, xr2, xg, in_l, pos_l, dgelu, grad_own,
    pm_sc, row_c, q_c, m_c,
    g_own, g_send, gc_recv, gy_send, gy_recv, gz_send, gz_recv,
    r_own, r_send, rc_recv, ry_send, ry_recv, rz_send, rz_recv,
    g_half, p_sc, pz_recv,
    xsem, zsem, ysem, csem,
):
    nx, ny, nz, nc, cap = dims
    b = lax.axis_index("bank")
    x = lax.axis_index("head")
    c = lax.rem(b, nc)
    z = lax.rem(b // nc, nz)
    y = b // (nc * nz)
    oc = 1 - c
    width = in_ref.shape[1]
    half = width // 2
    hidden_units = up_ref.shape[1]
    rows_own = bank_ref.shape[0]
    homes = home_ref.shape[1]
    gd_pieces = hidden_units // ny // 16
    block = nz

    def bid(yy, zz, cc):
        return (yy * nz + zz) * nc + cc

    def xdev(d):
        return (b, lax.rem(x + d, nx))

    def zdev(d):
        return (bid(y, lax.rem(z + d, nz), c), x)

    def ydev(d):
        return (bid(lax.rem(y + d, ny), z, c), x)

    cdev = (bid(y, z, oc), x)
    g_me = (c * ny + y) * nz + z

    def copy(src, dst, sems, i, dev):
        return pltpu.make_async_remote_copy(
            src_ref=src, dst_ref=dst, send_sem=sems.at[0, i], recv_sem=sems.at[1, i],
            device_id=dev, device_id_type=MESH,
        )

    def zloop(fn):
        def body(d, carry):
            fn(d)
            return carry
        lax.fori_loop(1, nz, body, 0)

    def zcopy(k, d, src, dst):
        return copy(src, dst, zsem, k * nz + d, zdev(d))

    def ycopy(k, d, src, dst):
        return copy(src, dst, ysem, k * ny + d, ydev(d))

    def ccopy(k, j, src, dst):
        return copy(src, dst, csem, k * ny + j, cdev)

    def xcopy(k, d, src, dst):
        return copy(src, dst, xsem, k * nx + d, xdev(d))

    barrier = pltpu.get_barrier_semaphore()
    pl.semaphore_signal(barrier, inc=1, device_id=cdev, device_id_type=MESH)
    for d in range(1, nx):
        pl.semaphore_signal(barrier, inc=1, device_id=xdev(d), device_id_type=MESH)
    for d in range(1, ny):
        pl.semaphore_signal(barrier, inc=1, device_id=ydev(d), device_id_type=MESH)
    zloop(lambda d: pl.semaphore_signal(barrier, inc=1, device_id=zdev(d), device_id_type=MESH))

    home = home_ref[...]
    part = iota((8, homes), 0)
    home8 = jnp.broadcast_to(home, (8, homes))
    table = jnp.where(part == 0, home8 >> 1, jnp.where(part == 1, home8 & 1, 0))
    table = table.astype(F32).astype(BF16)
    for i in range(PAIRS // 128):
        blocks = nb_ref[pl.ds(2 * x + i, 1), :]
        hot = jnp.where(iota((homes, 128), 0) == blocks, 1.0, 0.0).astype(BF16)
        found = dot(table, hot)
        place = 2.0 * found[0:1] + found[1:2]
        ids = place * float(BLOCK_ROWS) + nr_ref[pl.ds(2 * x + i, 1), :].astype(F32)
        meta_all[g_me, :, pl.ds(128 * i, 128)] = ids
        meta_all[g_me, :, pl.ds(PAIRS + 128 * i, 128)] = mg_ref[pl.ds(2 * x + i, 1), :]

    pl.semaphore_wait(barrier, (nx - 1) + (ny - 1) + (nz - 1) + 1)

    def own(ref, n=1):
        return ref.at[pl.ds(g_me, n)]

    zloop(lambda d: zcopy(0, d, own(meta_all), own(meta_all)).start())

    queries = in_ref[...]
    pre = dot(queries, up_ref[...]) + bias_ref[...]
    t = jnp.tanh(K0 * (pre + K1 * (pre * pre * pre)))
    hid = (0.5 * pre * (1.0 + t)).astype(BF16)
    h_all[y, c] = hid
    partial = dot(hid, down_ref[...])
    for i in range(nx):
        xs[i] = fold(partial[QH * i:QH * (i + 1)]).astype(BF16)
    for d in range(1, nx):
        xcopy(0, d, xs.at[lax.rem(x + d, nx)], xr.at[d]).start()
    ccopy(0, 0, h_all.at[y, c], h_all.at[y, c]).start()
    dgelu[...] = 0.5 * (1.0 + t) + 0.5 * pre * (1.0 - t * t) * (K0 * (1.0 + 3.0 * K1 * (pre * pre)))
    inf = queries.astype(F32)
    posf = pos_ref[...].astype(F32)
    for i in range(nx):
        in_l[i] = fold(inf[QH * i:QH * (i + 1)])
        pos_l[i] = fold(posf[QH * i:QH * (i + 1)])

    total = xs[x].astype(F32)
    for d in range(1, nx):
        xcopy(0, d, xs.at[0], xr.at[d]).wait_recv()
        total = total + xr[d].astype(F32)
    emb = (in_l[x] + total).astype(BF16)
    e_all[g_me] = emb
    s16 = jnp.sum(emb.astype(F32) * pos_l[x], axis=1, keepdims=True)
    s8 = s16[:QH] + s16[QH:]
    diag = iota((QH, 128), 0) == iota((QH, 128), 1)
    ps_all[g_me] = jnp.sum(jnp.where(diag, s8, 0.0), axis=0, keepdims=True)

    def send_emb(d):
        zcopy(1, d, own(e_all), own(e_all)).start()
        zcopy(2, d, own(ps_all), own(ps_all)).start()

    zloop(send_emb)

    ccopy(0, 0, h_all.at[y, c], h_all.at[y, oc]).wait_recv()
    for d in range(1, ny):
        ycopy(0, d, h_all.at[y], h_all.at[y]).start()

    zloop(lambda d: zcopy(0, d, own(meta_all), own(meta_all)).wait_recv())

    def ring(ref, cc, yy):
        return ref.at[pl.ds((cc * ny + yy) * nz, nz)]

    def yfrom(d):
        return lax.rem(y + ny - d, ny)

    for d in range(1, ny):
        ycopy(1, d, ring(meta_all, c, y), ring(meta_all, c, y)).start()
    ccopy(1, 0, ring(meta_all, c, y), ring(meta_all, c, y)).start()
    for d in range(1, ny):
        ycopy(1, d, ring(meta_all, c, y), ring(meta_all, c, yfrom(d))).wait_recv()
        ccopy(1, d, ring(meta_all, c, yfrom(d)), ring(meta_all, c, yfrom(d))).start()
    for d in range(ny):
        ccopy(1, d, ring(meta_all, c, y), ring(meta_all, oc, yfrom(d))).wait_recv()

    groups = meta_all.shape[0]
    ids = meta_all[:, 0, pl.ds(0, PAIRS)].astype(I32)
    margins = meta_all[:, 0, pl.ds(PAIRS, PAIRS)]
    owner = ids // rows_own
    local = (ids - owner * rows_own).astype(F32)
    mine = owner == b
    tri = jnp.where(iota((PAIRS, PAIRS), 0) <= iota((PAIRS, PAIRS), 1), 1.0, 0.0).astype(BF16)
    prefix = dot(jnp.where(mine, 1.0, 0.0).astype(BF16), tri)
    pm = jnp.where(mine, prefix, 0.0)
    pm_sc[...] = pm
    q_lane = (iota((groups, PAIRS), 1) // NEG + 1).astype(F32)
    for r in range(cap):
        sel = pm == float(r + 1)
        row_c[r] = jnp.sum(jnp.where(sel, local, 0.0), axis=1, keepdims=True)
        q_c[r] = jnp.sum(jnp.where(sel, q_lane, 0.0), axis=1, keepdims=True)
        m_c[r] = jnp.sum(jnp.where(sel, margins, 0.0), axis=1, keepdims=True)

    def wait_emb(d):
        zcopy(1, d, own(e_all), own(e_all)).wait_recv()
        zcopy(2, d, own(ps_all), own(ps_all)).wait_recv()

    zloop(wait_emb)
    for d in range(1, ny):
        ycopy(2, d, ring(e_all, c, y), ring(e_all, c, y)).start()
        ycopy(3, d, ring(ps_all, c, y), ring(ps_all, c, y)).start()
    ccopy(2, 0, ring(e_all, c, y), ring(e_all, c, y)).start()
    ccopy(3, 0, ring(ps_all, c, y), ring(ps_all, c, y)).start()
    for d in range(1, ny):
        src = yfrom(d)
        ycopy(2, d, ring(e_all, c, y), ring(e_all, c, src)).wait_recv()
        ycopy(3, d, ring(ps_all, c, y), ring(ps_all, c, src)).wait_recv()
        ccopy(2, d, ring(e_all, c, src), ring(e_all, c, src)).start()
        ccopy(3, d, ring(ps_all, c, src), ring(ps_all, c, src)).start()
    for d in range(ny):
        ccopy(2, d, ring(e_all, c, y), ring(e_all, oc, yfrom(d))).wait_recv()
        ccopy(3, d, ring(ps_all, c, y), ring(ps_all, oc, yfrom(d))).wait_recv()

    slots = cap * block
    ind = jnp.where(iota((PAIRS, 128), 0) // NEG == iota((PAIRS, 128), 1), 1.0, 0.0).astype(BF16)

    def score_block(cc, yy):
        first = pl.multiple_of((cc * ny + yy) * nz, nz)
        at = pl.ds(first, block)
        rows = jnp.concatenate([row_c[r, at, :] for r in range(cap)], axis=0)
        qs = jnp.concatenate([q_c[r, at, :] for r in range(cap)], axis=0)
        ms = jnp.concatenate([m_c[r, at, :] for r in range(cap)], axis=0)
        filled = qs > 0.5
        row_i = jnp.where(filled, rows, -1.0).astype(I32)
        hot_row = jnp.where(iota((slots, rows_own), 1) == row_i, 1.0, 0.0).astype(BF16)
        near = dot(hot_row, bank_ref[...])
        ps_rows = ps_all[at, 0, :]
        ps_rep = jnp.concatenate([ps_rows] * cap, axis=0)
        q_i = qs.astype(I32) - 1
        ps = jnp.sum(jnp.where(iota((slots, 128), 1) == q_i, ps_rep, 0.0), axis=1, keepdims=True)
        offs = (ps - ms).astype(BF16).astype(F32)
        group_i = lax.rem(iota((slots, 1), 0), block)
        target = jnp.where(filled, group_i * 16 + q_i, -100)
        target = jnp.concatenate([target, target + QH], axis=0)
        hot_q = jnp.where(iota((2 * slots, block * 16), 1) == target, 1.0, 0.0).astype(BF16)
        embs = dot(hot_q, e_all[at].reshape(block * 16, half))
        score = jnp.sum(
            embs[:slots] * near[:, :half] + embs[slots:] * near[:, half:], axis=1, keepdims=True
        )
        residual = offs - score
        weighted = (residual * near).astype(BF16)
        weighted = jnp.concatenate([weighted[:, :half], weighted[:, half:]], axis=0)
        summed = dot(hot_q, weighted, 0, 0).reshape(block, 16, half)
        rounded = residual.astype(BF16).astype(F32)
        pm_b = pm_sc[at, :]
        per_pair = jnp.zeros((block, PAIRS), F32)
        for r in range(cap):
            per_pair = per_pair + jnp.where(
                pm_b == float(r + 1), rounded[r * block:(r + 1) * block], 0.0
            )
        return summed, dot(per_pair.astype(BF16), ind)

    for d in range(ny):
        yy = lax.rem(y + d, ny)
        summed, rsum = score_block(oc, yy)
        g_send[yy] = summed.astype(BF16)
        r_send[yy, :, 0, :] = rsum
        ccopy(4, d, g_send.at[yy], gc_recv.at[yy]).start()
        ccopy(5, d, r_send.at[yy], rc_recv.at[yy]).start()
    for d in range(ny):
        yy = lax.rem(y + d, ny)
        summed, rsum = score_block(c, yy)
        g_own[yy] = summed
        r_own[yy, :, 0, :] = rsum

    def core_sum(d):
        yy = lax.rem(y + d, ny)
        ccopy(4, d, g_send.at[yy], gc_recv.at[yy]).wait_recv()
        ccopy(5, d, r_send.at[yy], rc_recv.at[yy]).wait_recv()
        return g_own[yy] + gc_recv[yy].astype(F32), r_own[yy] + rc_recv[yy]

    for d in range(1, ny):
        g_sum, r_sum = core_sum(d)
        gy_send[d] = g_sum.astype(BF16)
        ry_send[d] = r_sum
        ycopy(4, d, gy_send.at[d], gy_recv.at[d]).start()
        ycopy(5, d, ry_send.at[d], ry_recv.at[d]).start()
    g_sum, r_sum = core_sum(0)
    for d in range(1, ny):
        ycopy(4, d, gy_send.at[d], gy_recv.at[d]).wait_recv()
        ycopy(5, d, ry_send.at[d], ry_recv.at[d]).wait_recv()
        g_sum = g_sum + gy_recv[d].astype(F32)
        r_sum = r_sum + ry_recv[d]
    g_own[0] = g_sum
    rz_send[...] = r_sum
    gz_send[...] = g_sum.astype(BF16)

    def send_sum(d):
        zz = lax.rem(z + d, nz)
        zcopy(3, d, gz_send.at[zz], gz_recv.at[d]).start()
        zcopy(4, d, rz_send.at[zz], rz_recv.at[d]).start()

    zloop(send_sum)

    def add_sum(d, carry):
        zcopy(3, d, gz_send.at[0], gz_recv.at[d]).wait_recv()
        zcopy(4, d, rz_send.at[0], rz_recv.at[d]).wait_recv()
        return carry[0] + gz_recv[d].astype(F32), carry[1] + rz_recv[d]

    wsum, rsum = lax.fori_loop(1, nz, add_sum, (g_own[0, z], rz_send[z]))
    lane_q = iota((16, 128), 1) == lax.rem(iota((16, 128), 0), QH)
    rcol = jnp.sum(jnp.where(lane_q, rsum, 0.0), axis=1, keepdims=True)
    gradient = 2.0 * pos_l[x] * rcol - 2.0 * wsum
    grad_own[...] = gradient
    xg[x] = gradient.astype(BF16)
    for d in range(1, nx):
        xcopy(1, d, xg.at[x], xg.at[x]).start()
    for d in range(1, nx):
        src = lax.rem(x + nx - d, nx)
        xcopy(1, d, xg.at[x], xg.at[src]).wait_recv()

    pieces = [xg[i].astype(F32) for i in range(nx)]
    top = jnp.concatenate([p[:QH] for p in pieces], axis=0)
    low = jnp.concatenate([p[QH:] for p in pieces], axis=0)
    g_half[0] = top.astype(BF16)
    g_half[1] = low.astype(BF16)
    ccopy(6, 0, g_half.at[oc], f_all.at[y, c]).start()
    f_all[y, c] = g_half[c]
    ccopy(6, 0, g_half.at[oc], f_all.at[y, oc]).wait_recv()
    for d in range(1, ny):
        ycopy(6, d, f_all.at[y], f_all.at[y]).start()

    grad_all = jnp.concatenate([top, low], axis=1).astype(BF16)
    hidden_grad = dot(grad_all, down_ref[...], 1, 1)
    pre_grad = (hidden_grad * dgelu[...]).astype(BF16)
    carried = dot(pre_grad, up_ref[...], 1, 1)
    for i in range(nx):
        xs2[i] = fold(carried[QH * i:QH * (i + 1)]).astype(BF16)
    for d in range(1, nx):
        xcopy(2, d, xs2.at[lax.rem(x + d, nx)], xr2.at[d]).start()

    for d in range(1, ny):
        ycopy(0, d, h_all.at[y], h_all.at[yfrom(d)]).wait_recv()
        ycopy(6, d, f_all.at[y], f_all.at[yfrom(d)]).wait_recv()
    count = ny * nc * nx * QH
    down_sum = dot(
        h_all[...].reshape(count, hidden_units), f_all[...].reshape(count, half), 0, 0
    )
    p_sc[...] = down_sum.astype(BF16).reshape(ny * gd_pieces, 16, half)

    def send_down(d):
        zz = lax.rem(z + d, nz)

        @pl.when(zz < gd_pieces)
        def _():
            zcopy(5, d, p_sc.at[y * gd_pieces + zz], pz_recv.at[d]).start()

    zloop(send_down)
    scale = 1.0 / math.sqrt(nx * QH * ny * nz * nc)

    @pl.when(z < gd_pieces)
    def _():
        def add_down(d, carry):
            zcopy(5, d, p_sc.at[0], pz_recv.at[d]).wait_recv()
            return carry + pz_recv[d].astype(F32)

        acc = lax.fori_loop(1, nz, add_down, p_sc[y * gd_pieces + z].astype(F32))
        gd_all[c, y, z] = (acc * scale).astype(BF16)
        zloop(lambda d: zcopy(6, d, gd_all.at[c, y, z], gd_all.at[c, y, z]).start())

    carry = xs2[x].astype(F32) + grad_own[...]
    for d in range(1, nx):
        xcopy(2, d, xs2.at[0], xr2.at[d]).wait_recv()
        carry = carry + xr2[d].astype(F32)
    gi_ref[...] = unfold(carry).astype(BF16)

    def wait_down(d):
        zz = lax.rem(z + nz - d, nz)

        @pl.when(zz < gd_pieces)
        def _():
            zcopy(6, d, gd_all.at[c, y, 0], gd_all.at[c, y, zz]).wait_recv()

    zloop(wait_down)
    for d in range(1, ny):
        ycopy(7, d, gd_all.at[c, y], gd_all.at[c, y]).start()
    ccopy(7, 0, gd_all.at[c, y], gd_all.at[c, y]).start()
    for d in range(1, ny):
        src = yfrom(d)
        ycopy(7, d, gd_all.at[c, y], gd_all.at[c, src]).wait_recv()
        ccopy(7, d, gd_all.at[c, src], gd_all.at[c, src]).start()
    for d in range(ny):
        ccopy(7, d, gd_all.at[c, y], gd_all.at[oc, yfrom(d)]).wait_recv()
    for i in range(nc):
        gd_ref[:, half * i:half * (i + 1)] = gd_all[i].reshape(hidden_units, half)

    def sent(d):
        zz = lax.rem(z + d, nz)
        zcopy(0, d, own(meta_all), own(meta_all)).wait_send()
        zcopy(1, d, own(e_all), own(e_all)).wait_send()
        zcopy(2, d, own(ps_all), own(ps_all)).wait_send()
        zcopy(3, d, gz_send.at[0], gz_recv.at[d]).wait_send()
        zcopy(4, d, rz_send.at[0], rz_recv.at[d]).wait_send()

        @pl.when(zz < gd_pieces)
        def _():
            zcopy(5, d, p_sc.at[0], pz_recv.at[d]).wait_send()

        @pl.when(z < gd_pieces)
        def _():
            zcopy(6, d, gd_all.at[c, y, z], gd_all.at[c, y, z]).wait_send()

    zloop(sent)
    for d in range(1, nx):
        xcopy(0, d, xs.at[0], xr.at[d]).wait_send()
        xcopy(1, d, xg.at[x], xg.at[x]).wait_send()
        xcopy(2, d, xs2.at[0], xr2.at[d]).wait_send()
    for d in range(1, ny):
        ycopy(0, d, h_all.at[y], h_all.at[y]).wait_send()
        ycopy(1, d, ring(meta_all, c, y), ring(meta_all, c, y)).wait_send()
        ycopy(2, d, ring(e_all, c, y), ring(e_all, c, y)).wait_send()
        ycopy(3, d, ring(ps_all, c, y), ring(ps_all, c, y)).wait_send()
        ycopy(4, d, gy_send.at[d], gy_recv.at[d]).wait_send()
        ycopy(5, d, ry_send.at[d], ry_recv.at[d]).wait_send()
        ycopy(6, d, f_all.at[y], f_all.at[y]).wait_send()
        ycopy(7, d, gd_all.at[c, y], gd_all.at[c, y]).wait_send()
    ccopy(0, 0, h_all.at[y, c], h_all.at[y, c]).wait_send()
    ccopy(6, 0, g_half.at[oc], f_all.at[y, c]).wait_send()
    for d in range(ny):
        ccopy(1, d, ring(meta_all, c, y), ring(meta_all, c, y)).wait_send()
        ccopy(2, d, ring(e_all, c, y), ring(e_all, c, y)).wait_send()
        ccopy(3, d, ring(ps_all, c, y), ring(ps_all, c, y)).wait_send()
        ccopy(4, d, g_send.at[0], gc_recv.at[0]).wait_send()
        ccopy(5, d, r_send.at[0], rc_recv.at[0]).wait_send()
        ccopy(7, d, gd_all.at[c, y], gd_all.at[c, y]).wait_send()


def on_device(
    dims, inputs, positives, margins, neg_block, neg_row, block_home, bank, up_weight, up_bias,
    down_weight,
):
    nx, ny, nz, nc, cap = dims
    width = inputs.shape[1]
    half = width // 2
    units = up_weight.shape[1]
    queries = inputs.shape[0]
    groups = ny * nz * nc
    gd_pieces = units // ny // 16
    flat = (queries * NEG // 128, 128)
    V = pltpu.VMEM
    scratch = [
        V((groups, 1, 2 * PAIRS), F32),
        V((groups, 16, half), BF16),
        V((groups, 1, 128), F32),
        V((ny, nc, queries, units), BF16),
        V((ny, nc, queries, half), BF16),
        V((nc, ny, gd_pieces, 16, half), BF16),
        V((nx, 16, half), BF16),
        V((nx, 16, half), BF16),
        V((nx, 16, half), BF16),
        V((nx, 16, half), BF16),
        V((nx, 16, half), BF16),
        V((nx, 16, half), F32),
        V((nx, 16, half), F32),
        V((queries, units), F32),
        V((16, half), F32),
        V((groups, PAIRS), F32),
        V((cap, groups, 1), F32),
        V((cap, groups, 1), F32),
        V((cap, groups, 1), F32),
        V((ny, nz, 16, half), F32),
        V((ny, nz, 16, half), BF16),
        V((ny, nz, 16, half), BF16),
        V((ny, nz, 16, half), BF16),
        V((ny, nz, 16, half), BF16),
        V((nz, 16, half), BF16),
        V((nz, 16, half), BF16),
        V((ny, nz, 1, 128), F32),
        V((ny, nz, 1, 128), F32),
        V((ny, nz, 1, 128), F32),
        V((ny, nz, 1, 128), F32),
        V((ny, nz, 1, 128), F32),
        V((nz, 1, 128), F32),
        V((nz, 1, 128), F32),
        V((nc, queries, half), BF16),
        V((ny * gd_pieces, 16, half), BF16),
        V((nz, 16, half), BF16),
        pltpu.SemaphoreType.DMA((2, 3 * nx)),
        pltpu.SemaphoreType.DMA((2, 7 * nz)),
        pltpu.SemaphoreType.DMA((2, 8 * ny)),
        pltpu.SemaphoreType.DMA((2, 8 * ny)),
    ]
    vmem = pl.BlockSpec(memory_space=pltpu.VMEM)
    return pl.pallas_call(
        functools.partial(kernel, dims),
        out_shape=(
            jax.ShapeDtypeStruct((QH, width), BF16),
            jax.ShapeDtypeStruct((units, width), BF16),
        ),
        in_specs=[vmem] * 10,
        out_specs=(vmem, vmem),
        scratch_shapes=scratch,
        compiler_params=pltpu.CompilerParams(
            collective_id=0, has_side_effects=True, vmem_limit_bytes=40 * 1024 * 1024
        ),
        cost_estimate=pl.CostEstimate(
            flops=4_000_000_000, bytes_accessed=6_000_000, transcendentals=30_000
        ),
    )(
        inputs, positives, neg_block.reshape(flat), neg_row.reshape(flat), margins.reshape(flat),
        block_home.reshape(1, -1), bank, up_weight, up_bias.reshape(1, -1), down_weight,
    )


def solution(mesh, ny=4, nc=2, cap=4):
    nx = mesh.shape["head"]
    nz = mesh.shape["bank"] // (ny * nc)
    return jax.shard_map(
        functools.partial(on_device, (nx, ny, nz, nc, cap)),
        mesh=mesh,
        in_specs=(
            P("bank", None),
            P("bank", None),
            P("bank", None),
            P("bank", None),
            P("bank", None),
            P(),
            P("bank", None),
            P(None, "head"),
            P("head"),
            P("head", None),
        ),
        out_specs=(P(("bank", "head"), None), P("head", None)),
        check_vma=False,
    )
```

time: 596 us -> 134 us (0.22)
  waiting for transfers between devices: 459 us -> 0 us
  Pallas kernels: 0 us -> 122 us
  starting transfers between devices: 56.7 us -> 0 us
  blocking collectives: 23.6 us -> 0 us
  between operations: 15.8 us -> 0.65 us
  local copies, waits for them, and re-layouts: 23 us -> 10.6 us
  other arithmetic: 11.8 us -> 0 us
    psum x1 -> x0, waiting for transfers between devices: 326 us -> none  [on_device(): summed = lax.psum(local_down, 'bank')]
    pallas_call x0 -> x1, Pallas kernels: none -> 122 us  [on_device(): pl.pallas_call(functools.partial(kernel, dims), out_shape=(jax.ShapeDtype...]
    all_to_all x5 -> x0, waiting for transfers between devices: 114 us -> none  [the longest x1 43.1 us: on_device(): lax.all_to_all(weighted_part, 'bank', split_axis=0, concat_axis=0, tiled=...]
    all_to_all x5 -> x0, starting transfers between devices: 56.6 us -> none  [the longest x1 23.3 us: on_device(): lax.all_to_all(sent_offsets.reshape(grid_shape), 'bank', split_axis=0, co...]
    reduce_scatter x1 -> x0, waiting for transfers between devices: 18 us -> none  [on_device(): lax.psum_scatter(lax.dot_general(pre_grad, up_weight, (((1,), (1,)), ((),...]
    gather x8 -> x0, local copies, waits for them, and re-layouts: 17.7 us -> none  [the longest x2 4.39 us: on_device(): neighbours = bank[row_part]]
    psum x1 -> x0, blocking collectives: 14.6 us -> none  [on_device(): lax.psum(partial_emb.astype(jnp.bfloat16), 'head').astype(jnp.float32)]
    all_gather x1 -> x0, blocking collectives: 9.02 us -> none  [on_device(): grad_all = lax.all_gather(grad_rounded, 'head', axis=0, tiled=True)]
  transfers between devices with their start and end apart: 7 -> 0, of which waited for: 7 -> 0; matrix products, arithmetic and copies ran while one was open for 3% -> 0% of each run, Pallas kernels for 0% -> 0%
where the time goes in v1:
time: 134 us
  Pallas kernels  122 us (91%)
  local copies, waits for them, and re-layouts  10.6 us (8%)
    pallas_call x1, Pallas kernels, on_device(): pl.pallas_call(functools.partial(kernel, dims), out_shape=(jax.ShapeDtype...  122 us
    unnamed x14, local copies, waits for them, and re-layouts  7.57 us

profile of v1, /device:TPU:1, one launch (start us, length us, event | category | flops | bytes accessed | tf_op | source)
XLA Modules:
  0.0 133.6 jit_solution(15092014031759010810)
XLA Ops:
  0.6 0.7 reshape.23.bias_ref
  1.3 0.8 reshape.21.mg_ref
  2.1 0.8 reshape.19.nb_ref
  2.9 0.8 reshape.20.nr_ref
  3.7 0.0 copy-start
  3.7 1.3 copy-done
  5.0 0.0 copy-start.1
  5.0 1.3 copy-done.1
  6.2 0.0 copy-start.2
  6.2 1.1 copy-done.2
  7.4 0.0 copy-start.3
  7.4 0.8 copy-done.3
  8.2 0.0 copy-start.4
  8.2 0.8 copy-done.4
  9.0 0.0 copy-start.5
  9.0 0.7 copy-done.5
  9.6 122.3 %shard_map.113 = (bf16[8,768]{1,0:T(8,128)(2,1)S(1)}, bf16[768,768]{1,0:T(8,128)(2,1)S(1)}) custom-call(bf16[32,768]{1,0:T(8,128)(2,1)S(1)} %copy-done.3, bf16[32,768]{1,0:T(8,128)(2,1)S(1)} %copy-done.4, s32[8,128]{1,0:T(8,128)S(1)} %reshape.19.nb_ref, s32[8,128]{1,0:T(8,128)S(1)} %reshape.20.nr_ref, f32[8,128]{1,0:T(8,128)S(1)} %reshape.21.mg_ref, ...), custom_call_target="tpu_custom_call" | custom-call | flops 4000000000 | bytes 6000000 | tf_op jit(solution)/shard_map/pallas_call | solution.py:498
  132.0 0.6 copy.14
  132.6 1.0 copy.15
Async XLA Ops:
  3.7 1.3 copy-start
  5.0 1.3 copy-start.1
  6.2 1.1 copy-start.2
  7.4 0.8 copy-start.3
  8.2 0.8 copy-start.4
  9.0 0.7 copy-start.5

commit v2 on v0

v2 whole, which is shorter than its diff:
```python
import functools
import math

import jax
import jax.numpy as jnp
from jax import lax
from jax.experimental import pallas as pl
from jax.experimental.pallas import tpu as pltpu
from jax.sharding import PartitionSpec as P

MESH = pl.DeviceIdType.MESH
F32 = jnp.float32
BF16 = jnp.bfloat16
I32 = jnp.int32
NEG = 32
BLOCK_ROWS = 128
QH = 8
PAIRS = QH * NEG
K0 = math.sqrt(2.0 / math.pi)
K1 = 0.044715


def iota(shape, axis):
    return lax.broadcasted_iota(I32, shape, axis)


def dot(a, b, ca=1, cb=0):
    return lax.dot_general(a, b, (((ca,), (cb,)), ((), ())), preferred_element_type=F32)


def fold(rows):
    w = rows.shape[1] // 2
    return jnp.concatenate([rows[:, :w], rows[:, w:]], axis=0)


def unfold(rows):
    return jnp.concatenate([rows[:QH], rows[QH:]], axis=1)


def kernel(
    dims,
    in_hbm, pos_hbm, nb_hbm, nr_hbm, mg_hbm, home_hbm, bank_hbm, up_hbm, bias_hbm, down_hbm,
    gi_ref, gd_ref,
    in_ref, pos_ref, nb_ref, nr_ref, mg_ref, home_ref, bank_ref, up_ref, bias_ref, down_ref,
    meta_all, e_all, ps_all, h_all, f_all, gd_all,
    xs, xr, xs2, xr2, xg, in_l, pos_l, dgelu,
    pm_sc, near_sc, q_sc, m_sc,
    g_own, g_send, gc_recv, gy_send, gy_recv, gz_send, gz_recv,
    r_own, r_send, rc_recv, ry_send, ry_recv, rz_send, rz_recv,
    p_sc, pz_recv,
    lsem, xsem, zsem, ysem, csem,
):
    nx, ny, nz, nc, cap = dims
    per = min(4, nz)
    chunks = nz // per
    rings = ny * per
    block = nc * rings
    slots = cap * block
    b = lax.axis_index("bank")
    x = lax.axis_index("head")
    c = lax.rem(b, nc)
    z = lax.rem(b // nc, nz)
    y = b // (nc * nz)
    oc = 1 - c
    width = in_ref.shape[1]
    half = width // 2
    units = up_ref.shape[1]
    rows_own = bank_ref.shape[0]
    homes = home_ref.shape[1]
    gd_pieces = units // ny // 16
    offs = [(s + 1) // 2 if s % 2 else -(s // 2) for s in range(nz)]

    def bid(yy, zz, cc):
        return (yy * nz + zz) * nc + cc

    def zat(off):
        return lax.rem(z + (off + nz), nz)

    def xdev(d):
        return (b, lax.rem(x + d, nx))

    def xcdev(d):
        return (bid(y, z, oc), lax.rem(x + d, nx))

    def zdev(off):
        return (bid(y, zat(off), c), x)

    def ydev(d):
        return (bid(lax.rem(y + d, ny), z, c), x)

    cdev = xcdev(0)
    unsent = []

    def copy(src, dst, sems, i, dev):
        return pltpu.make_async_remote_copy(
            src_ref=src, dst_ref=dst, send_sem=sems.at[0, i], recv_sem=sems.at[1, i],
            device_id=dev, device_id_type=MESH,
        )

    def start(cp, when=None):
        if when is None:
            cp.start()
        else:
            pl.when(when)(cp.start)
        unsent.append((cp, when))

    def zcopy(k, s, off, src, dst):
        return copy(src, dst, zsem, k * nz + s, zdev(off))

    def ycopy(k, d, src, dst):
        return copy(src, dst, ysem, k * ny + d, ydev(d))

    def ccopy(k, src, dst):
        return copy(src, dst, csem, k, cdev)

    def xcopy(k, d, src, dst):
        return copy(src, dst, xsem, k * nx + d, xdev(d))

    pairs = [
        (nb_hbm, nb_ref), (nr_hbm, nr_ref), (mg_hbm, mg_ref), (home_hbm, home_ref),
        (in_hbm, in_ref), (up_hbm, up_ref), (bias_hbm, bias_ref), (down_hbm, down_ref),
        (pos_hbm, pos_ref), (bank_hbm, bank_ref),
    ]
    loads = [pltpu.make_async_copy(src, dst, lsem.at[i]) for i, (src, dst) in enumerate(pairs)]
    for cp in loads:
        cp.start()

    barrier = pltpu.get_barrier_semaphore()
    greet = [xcdev(d) for d in range(nx)] + [xdev(d) for d in range(1, nx)]
    greet += [ydev(d) for d in range(1, ny)] + [zdev(o) for o in offs[1:]]
    for dev in greet:
        pl.semaphore_signal(barrier, inc=1, device_id=dev, device_id_type=MESH)

    for cp in loads[:4]:
        cp.wait()
    mine8 = pl.ds(pl.multiple_of(x * QH, QH), QH)
    lanes = 128 // NEG

    def row_of(rows, i):
        return jnp.concatenate([rows[lanes * i + k:lanes * i + k + 1] for k in range(lanes)], axis=1)

    home = home_ref[...]
    part = iota((8, homes), 0)
    home8 = jnp.broadcast_to(home, (8, homes))
    table = jnp.where(part == 0, home8 >> 1, jnp.where(part == 1, home8 & 1, 0))
    table = table.astype(F32).astype(BF16)
    nb8, nr8, mg8 = nb_ref[mine8, :], nr_ref[mine8, :], mg_ref[mine8, :]
    for i in range(PAIRS // 128):
        hot = jnp.where(iota((homes, 128), 0) == row_of(nb8, i), 1.0, 0.0).astype(BF16)
        found = dot(table, hot)
        place = 2.0 * found[0:1] + found[1:2]
        ids = place * float(BLOCK_ROWS) + row_of(nr8, i).astype(F32)
        meta_all[0, 0, :, pl.ds(128 * i, 128)] = ids
        meta_all[0, 0, :, pl.ds(PAIRS + 128 * i, 128)] = row_of(mg8, i)

    pl.semaphore_wait(barrier, len(greet))

    far_first = list(range(nz - 1, 0, -1))

    def zgather(k, s, ref):
        return zcopy(k, s, -offs[s], ref.at[0, pl.ds(0, 1)], ref.at[s // per, pl.ds(s % per, 1)])

    for s in far_first:
        start(zgather(0, s, meta_all))

    for cp in loads[4:8]:
        cp.wait()
    queries = in_ref[...]
    pre = dot(queries, up_ref[...]) + bias_ref[...]
    t = jnp.tanh(K0 * (pre + K1 * (pre * pre * pre)))
    hid = (0.5 * pre * (1.0 + t)).astype(BF16)
    h_all[0, 0] = hid
    partial = dot(hid, down_ref[...])
    for i in range(nx):
        xs[i] = fold(partial[QH * i:QH * (i + 1)]).astype(BF16)
    for d in range(1, nx):
        start(xcopy(0, d, xs.at[lax.rem(x + d, nx)], xr.at[d]))
    start(ccopy(0, h_all.at[0, 0], h_all.at[0, 1]))
    dgelu[...] = 0.5 * (1.0 + t) + 0.5 * pre * (1.0 - t * t) * (K0 * (1.0 + 3.0 * K1 * (pre * pre)))
    inf = queries.astype(F32)
    loads[8].wait()
    posf = pos_ref[...].astype(F32)
    for i in range(nx):
        in_l[i] = fold(inf[QH * i:QH * (i + 1)])
        pos_l[i] = fold(posf[QH * i:QH * (i + 1)])

    total = xs[x].astype(F32)
    for d in range(1, nx):
        xcopy(0, d, xs.at[0], xr.at[d]).wait_recv()
        total = total + xr[d].astype(F32)
    emb = (in_l[x] + total).astype(BF16)
    e_all[0, 0] = emb
    s16 = jnp.sum(emb.astype(F32) * pos_l[x], axis=1, keepdims=True)
    s8 = s16[:QH] + s16[QH:]
    diag = iota((QH, 128), 0) == iota((QH, 128), 1)
    ps_all[0, 0] = jnp.sum(jnp.where(diag, s8, 0.0), axis=0, keepdims=True)
    for s in far_first:
        start(zgather(1, s, e_all))
        start(zgather(2, s, ps_all))

    def near_ring(ref, k, d=0):
        return ref.at[k, pl.ds(d * per, per)]

    def emb_z(k):
        for s in range(max(1, k * per), (k + 1) * per):
            zgather(1, s, e_all).wait_recv()
            zgather(2, s, ps_all).wait_recv()
        for d in range(1, ny):
            start(ycopy(2 + k, d, near_ring(e_all, k), near_ring(e_all, k, ny - d)))
            start(ycopy(6 + k, d, near_ring(ps_all, k), near_ring(ps_all, k, ny - d)))

    def emb_y(k):
        for d in range(1, ny):
            ycopy(2 + k, d, near_ring(e_all, k), near_ring(e_all, k, ny - d)).wait_recv()
            ycopy(6 + k, d, near_ring(ps_all, k), near_ring(ps_all, k, ny - d)).wait_recv()
        start(emb_core(2 + k, e_all, k))
        start(emb_core(6 + k, ps_all, k))

    def emb_core(i, ref, k):
        return ccopy(i, ref.at[k, pl.ds(0, rings)], ref.at[k, pl.ds(rings, rings)])

    for s in range(1, nz):
        zgather(0, s, meta_all).wait_recv()

    def meta_y(d):
        return ycopy(
            1, d, meta_all.at[:, pl.ds(0, per)], meta_all.at[:, pl.ds((ny - d) * per, per)]
        )

    for d in range(1, ny):
        start(meta_y(d))
    ccopy(0, h_all.at[0, 0], h_all.at[0, 1]).wait_recv()
    for d in range(1, ny):
        meta_y(d).wait_recv()
    meta_c = ccopy(1, meta_all.at[:, pl.ds(0, rings)], meta_all.at[:, pl.ds(rings, rings)])
    start(meta_c)
    emb_z(0)
    meta_c.wait_recv()
    loads[9].wait()

    tri = jnp.where(iota((PAIRS, PAIRS), 0) <= iota((PAIRS, PAIRS), 1), 1.0, 0.0).astype(BF16)
    q_lane = (iota((block, PAIRS), 1) // NEG + 1).astype(F32)
    for k in range(chunks):
        ids = meta_all[k, :, 0, pl.ds(0, PAIRS)].astype(I32)
        margins = meta_all[k, :, 0, pl.ds(PAIRS, PAIRS)]
        owner = ids // rows_own
        local = (ids - owner * rows_own).astype(F32)
        mine = owner == b
        prefix = dot(jnp.where(mine, 1.0, 0.0).astype(BF16), tri)
        pm = jnp.where(mine, prefix, 0.0)
        pm_sc[k] = pm
        rows, qs, ms = [], [], []
        for r in range(cap):
            sel = pm == float(r + 1)
            rows.append(jnp.sum(jnp.where(sel, local, 0.0), axis=1, keepdims=True))
            qs.append(jnp.sum(jnp.where(sel, q_lane, 0.0), axis=1, keepdims=True))
            ms.append(jnp.sum(jnp.where(sel, margins, 0.0), axis=1, keepdims=True))
        rows, qs = jnp.concatenate(rows, axis=0), jnp.concatenate(qs, axis=0)
        q_sc[k] = qs
        m_sc[k] = jnp.concatenate(ms, axis=0)
        row_i = jnp.where(qs > 0.5, rows, -1.0).astype(I32)
        hot_row = jnp.where(iota((slots, rows_own), 1) == row_i, 1.0, 0.0).astype(BF16)
        near_sc[k] = dot(hot_row, bank_ref[...]).astype(BF16)

    ind = jnp.where(iota((PAIRS, 128), 0) // NEG == iota((PAIRS, 128), 1), 1.0, 0.0).astype(BF16)

    def score(k):
        emb_core(2 + k, e_all, k).wait_recv()
        emb_core(6 + k, ps_all, k).wait_recv()
        qs = q_sc[k]
        q_i = qs.astype(I32) - 1
        ps_rep = jnp.concatenate([ps_all[k, :, 0, :]] * cap, axis=0)
        ps = jnp.sum(jnp.where(iota((slots, 128), 1) == q_i, ps_rep, 0.0), axis=1, keepdims=True)
        offsets = (ps - m_sc[k]).astype(BF16).astype(F32)
        group_i = lax.rem(iota((slots, 1), 0), block)
        target = jnp.where(qs > 0.5, group_i * 16 + q_i, -100)
        target = jnp.concatenate([target, target + QH], axis=0)
        hot_q = jnp.where(iota((2 * slots, block * 16), 1) == target, 1.0, 0.0).astype(BF16)
        embs = dot(hot_q, e_all[k].reshape(block * 16, half))
        near = near_sc[k].astype(F32)
        found = jnp.sum(
            embs[:slots] * near[:, :half] + embs[slots:] * near[:, half:], axis=1, keepdims=True
        )
        residual = offsets - found
        weighted = (residual * near).astype(BF16)
        weighted = jnp.concatenate([weighted[:, :half], weighted[:, half:]], axis=0)
        summed = dot(hot_q, weighted, 0, 0).reshape(block, 16, half)
        rounded = residual.astype(BF16).astype(F32)
        pm = pm_sc[k]
        per_pair = jnp.zeros((block, PAIRS), F32)
        for r in range(cap):
            per_pair = per_pair + jnp.where(
                pm == float(r + 1), rounded[r * block:(r + 1) * block], 0.0
            )
        rsum = dot(per_pair.astype(BF16), ind)
        g_send[k] = summed[rings:].astype(BF16)
        r_send[k, :, 0, :] = rsum[rings:]
        start(ccopy(10 + k, g_send.at[k], gc_recv.at[k]))
        start(ccopy(14 + k, r_send.at[k], rc_recv.at[k]))
        g_own[k] = summed[:rings]
        r_own[k, :, 0, :] = rsum[:rings]

    def sum_core(k):
        ccopy(10 + k, g_send.at[k], gc_recv.at[k]).wait_recv()
        ccopy(14 + k, r_send.at[k], rc_recv.at[k]).wait_recv()
        for d in list(range(1, ny)) + [0]:
            at = pl.ds(d * per, per)
            g_sum = g_own[k, at] + gc_recv[k, at].astype(F32)
            r_sum = r_own[k, at] + rc_recv[k, at]
            if d:
                gy_send[k, d] = g_sum.astype(BF16)
                ry_send[k, d] = r_sum
                start(ycopy(10 + k, d, gy_send.at[k, d], gy_recv.at[k, d]))
                start(ycopy(14 + k, d, ry_send.at[k, d], ry_recv.at[k, d]))
            else:
                g_own[k, at] = g_sum
                r_own[k, at] = r_sum

    def sum_y(k):
        g_sum = g_own[k, pl.ds(0, per)]
        r_sum = r_own[k, pl.ds(0, per)]
        for d in range(1, ny):
            ycopy(10 + k, d, gy_send.at[k, d], gy_recv.at[k, d]).wait_recv()
            ycopy(14 + k, d, ry_send.at[k, d], ry_recv.at[k, d]).wait_recv()
            g_sum = g_sum + gy_recv[k, d].astype(F32)
            r_sum = r_sum + ry_recv[k, d]
        gz_send[k] = g_sum.astype(BF16)
        rz_send[k] = r_sum
        if k == 0:
            g_own[0, 0] = g_sum[0]
        for s in range((k + 1) * per - 1, max(1, k * per) - 1, -1):
            start(zcopy(3, s, offs[s], gz_send.at[k, s % per], gz_recv.at[s]))
            start(zcopy(4, s, offs[s], rz_send.at[k, s % per], rz_recv.at[s]))

    def hidden_y():
        for d in range(1, ny):
            start(ycopy(0, d, h_all.at[0], h_all.at[ny - d]))

    stages = [emb_z, emb_y, score, sum_core, sum_y]
    lag = [0, 1, 2, 3, 4]
    for step in range(1, chunks + len(stages) - 1):
        for stage, late in zip(stages, lag):
            if 0 <= step - late < chunks:
                stage(step - late)
        if step == chunks:
            hidden_y()
    if chunks + len(stages) - 2 < chunks:
        hidden_y()

    wsum = g_own[0, 0]
    rsum = rz_send[0, 0]
    for s in range(1, nz):
        zcopy(3, s, offs[s], gz_send.at[0, 0], gz_recv.at[s]).wait_recv()
        zcopy(4, s, offs[s], rz_send.at[0, 0], rz_recv.at[s]).wait_recv()
        wsum = wsum + gz_recv[s].astype(F32)
        rsum = rsum + rz_recv[s]
    lane_q = iota((16, 128), 1) == lax.rem(iota((16, 128), 0), QH)
    rcol = jnp.sum(jnp.where(lane_q, rsum, 0.0), axis=1, keepdims=True)
    gradient = 2.0 * pos_l[x] * rcol - 2.0 * wsum
    xg[0, x] = gradient.astype(BF16)
    for d in range(1, nx):
        start(xcopy(1, d, xg.at[0, x], xg.at[0, x]))
    for d in range(nx):
        start(copy(xg.at[0, x], xg.at[1, x], xsem, 3 * nx + d, xcdev(d)))
    for d in range(nx):
        src = lax.rem(x + nx - d, nx)
        if d:
            xcopy(1, d, xg.at[0, x], xg.at[0, src]).wait_recv()
        copy(xg.at[0, x], xg.at[1, src], xsem, 3 * nx + d, xcdev(d)).wait_recv()

    def halves(cr):
        pieces = [xg[cr, i].astype(F32) for i in range(nx)]
        top = jnp.concatenate([p[:QH] for p in pieces], axis=0)
        low = jnp.concatenate([p[QH:] for p in pieces], axis=0)
        f_all[0, cr] = jnp.where(c == 0, top, low).astype(BF16)
        return top, low

    top, low = halves(0)
    halves(1)
    for d in range(1, ny):
        start(ycopy(18, d, f_all.at[0], f_all.at[ny - d]))

    grad_all = jnp.concatenate([top, low], axis=1).astype(BF16)
    hidden_grad = dot(grad_all, down_ref[...], 1, 1)
    pre_grad = (hidden_grad * dgelu[...]).astype(BF16)
    carried = dot(pre_grad, up_ref[...], 1, 1)
    for i in range(nx):
        xs2[i] = fold(carried[QH * i:QH * (i + 1)]).astype(BF16)
    for d in range(1, nx):
        start(xcopy(2, d, xs2.at[lax.rem(x + d, nx)], xr2.at[d]))

    for d in range(1, ny):
        ycopy(0, d, h_all.at[0], h_all.at[ny - d]).wait_recv()
        ycopy(18, d, f_all.at[0], f_all.at[ny - d]).wait_recv()
    count = ny * nc * nx * QH
    down_sum = dot(h_all[...].reshape(count, units), f_all[...].reshape(count, half), 0, 0)
    p_sc[...] = down_sum.astype(BF16).reshape(ny * gd_pieces, 16, half)
    for s in far_first:
        zz = zat(offs[s])
        piece = p_sc.at[y * gd_pieces + jnp.minimum(zz, gd_pieces - 1)]
        start(zcopy(5, s, offs[s], piece, pz_recv.at[s]), zz < gd_pieces)

    carry = xs2[x].astype(F32) + gradient
    for d in range(1, nx):
        xcopy(2, d, xs2.at[0], xr2.at[d]).wait_recv()
        carry = carry + xr2[d].astype(F32)
    gi_ref[...] = unfold(carry).astype(BF16)

    busy = z < gd_pieces
    scale = 1.0 / math.sqrt(nx * QH * ny * nz * nc)

    @pl.when(busy)
    def _():
        acc = p_sc[y * gd_pieces + jnp.minimum(z, gd_pieces - 1)].astype(F32)
        for s in range(1, nz):
            zcopy(5, s, offs[s], p_sc.at[0], pz_recv.at[s]).wait_recv()
            acc = acc + pz_recv[s].astype(F32)
        gd_all[0, 0] = (acc * scale).astype(BF16)

    def zlast(s):
        return zgather(6, s, gd_all)

    for s in far_first:
        start(zlast(s), busy)

    def last_z(k):
        for s in range(max(1, k * per), (k + 1) * per):
            pl.when(zat(offs[s]) < gd_pieces)(zlast(s).wait_recv)
        for d in range(1, ny):
            start(ycopy(19 + k, d, near_ring(gd_all, k), near_ring(gd_all, k, ny - d)))

    def last_y(k):
        for d in range(1, ny):
            ycopy(19 + k, d, near_ring(gd_all, k), near_ring(gd_all, k, ny - d)).wait_recv()
        start(emb_core(18 + k, gd_all, k))
        put(k, 0)

    def put(k, cr):
        at = c if cr == 0 else oc
        for s in range(per):
            zz = zat(offs[k * per + s])

            @pl.when(zz < gd_pieces)
            def _():
                for d in range(ny):
                    yy = lax.rem(y + d, ny)
                    row = pl.multiple_of((yy * gd_pieces + zz) * 16, 16)
                    col = pl.multiple_of(at * half, 128)
                    gd_ref[pl.ds(row, 16), pl.ds(col, half)] = gd_all[k, cr * rings + d * per + s]

    def last_core(k):
        emb_core(18 + k, gd_all, k).wait_recv()
        put(k, 1)

    stages = [last_z, last_y, last_core]
    for step in range(chunks + len(stages) - 1):
        for late, stage in enumerate(stages):
            if 0 <= step - late < chunks:
                stage(step - late)

    for cp, when in unsent:
        if when is None:
            cp.wait_send()
        else:
            pl.when(when)(cp.wait_send)


def on_device(
    dims, inputs, positives, margins, neg_block, neg_row, block_home, bank, up_weight, up_bias,
    down_weight,
):
    nx, ny, nz, nc, cap = dims
    width = inputs.shape[1]
    half = width // 2
    units = up_weight.shape[1]
    queries = inputs.shape[0]
    per = min(4, nz)
    chunks = nz // per
    rings = ny * per
    block = nc * rings
    slots = cap * block
    gd_pieces = units // ny // 16
    V = pltpu.VMEM
    args = (
        inputs, positives, neg_block, neg_row, margins, block_home.reshape(1, -1), bank,
        up_weight, up_bias.reshape(1, -1), down_weight,
    )
    scratch = [V(a.shape, a.dtype) for a in args] + [
        V((chunks, block, 1, 2 * PAIRS), F32),
        V((chunks, block, 16, half), BF16),
        V((chunks, block, 1, 128), F32),
        V((ny, nc, queries, units), BF16),
        V((ny, nc, queries, half), BF16),
        V((chunks, block, 16, half), BF16),
        V((nx, 16, half), BF16),
        V((nx, 16, half), BF16),
        V((nx, 16, half), BF16),
        V((nx, 16, half), BF16),
        V((nc, nx, 16, half), BF16),
        V((nx, 16, half), F32),
        V((nx, 16, half), F32),
        V((queries, units), F32),
        V((chunks, block, PAIRS), F32),
        V((chunks, slots, width), BF16),
        V((chunks, slots, 1), F32),
        V((chunks, slots, 1), F32),
        V((chunks, rings, 16, half), F32),
        V((chunks, rings, 16, half), BF16),
        V((chunks, rings, 16, half), BF16),
        V((chunks, ny, per, 16, half), BF16),
        V((chunks, ny, per, 16, half), BF16),
        V((chunks, per, 16, half), BF16),
        V((nz, 16, half), BF16),
        V((chunks, rings, 1, 128), F32),
        V((chunks, rings, 1, 128), F32),
        V((chunks, rings, 1, 128), F32),
        V((chunks, ny, per, 1, 128), F32),
        V((chunks, ny, per, 1, 128), F32),
        V((chunks, per, 1, 128), F32),
        V((nz, 1, 128), F32),
        V((ny * gd_pieces, 16, half), BF16),
        V((nz, 16, half), BF16),
        pltpu.SemaphoreType.DMA((len(args),)),
        pltpu.SemaphoreType.DMA((2, 4 * nx)),
        pltpu.SemaphoreType.DMA((2, 7 * nz)),
        pltpu.SemaphoreType.DMA((2, 23 * ny)),
        pltpu.SemaphoreType.DMA((2, 22)),
    ]
    vmem = pl.BlockSpec(memory_space=pltpu.VMEM)
    return pl.pallas_call(
        functools.partial(kernel, dims),
        out_shape=(
            jax.ShapeDtypeStruct((QH, width), BF16),
            jax.ShapeDtypeStruct((units, width), BF16),
        ),
        in_specs=[pl.BlockSpec(memory_space=pltpu.HBM)] * len(args),
        out_specs=(vmem, vmem),
        scratch_shapes=scratch,
        compiler_params=pltpu.CompilerParams(
            collective_id=0, has_side_effects=True, vmem_limit_bytes=40 * 1024 * 1024
        ),
        cost_estimate=pl.CostEstimate(
            flops=4_000_000_000, bytes_accessed=6_000_000, transcendentals=30_000
        ),
    )(*args)


def solution(mesh, ny=4, nc=2, cap=4):
    nx = mesh.shape["head"]
    nz = mesh.shape["bank"] // (ny * nc)
    return jax.shard_map(
        functools.partial(on_device, (nx, ny, nz, nc, cap)),
        mesh=mesh,
        in_specs=(
            P("bank", None),
            P("bank", None),
            P("bank", None),
            P("bank", None),
            P("bank", None),
            P(),
            P("bank", None),
            P(None, "head"),
            P("head"),
            P("head", None),
        ),
        out_specs=(P(("bank", "head"), None), P("head", None)),
        check_vma=False,
    )
```

time: 596 us -> 126 us (0.21)
  waiting for transfers between devices: 459 us -> 0 us
  Pallas kernels: 0 us -> 114 us
  starting transfers between devices: 56.7 us -> 0 us
  blocking collectives: 23.6 us -> 0 us
  between operations: 15.8 us -> 0.65 us
  local copies, waits for them, and re-layouts: 23 us -> 10.4 us
  other arithmetic: 11.8 us -> 0 us
    psum x1 -> x0, waiting for transfers between devices: 326 us -> none  [on_device(): summed = lax.psum(local_down, 'bank')]
    all_to_all x5 -> x0, waiting for transfers between devices: 114 us -> none  [the longest x1 43.1 us: on_device(): lax.all_to_all(weighted_part, 'bank', split_axis=0, concat_axis=0, tiled=...]
    pallas_call x0 -> x1, Pallas kernels: none -> 114 us  [on_device(): pl.pallas_call(functools.partial(kernel, dims), out_shape=(jax.ShapeDtype...]
    all_to_all x5 -> x0, starting transfers between devices: 56.6 us -> none  [the longest x1 23.3 us: on_device(): lax.all_to_all(sent_offsets.reshape(grid_shape), 'bank', split_axis=0, co...]
    reduce_scatter x1 -> x0, waiting for transfers between devices: 18 us -> none  [on_device(): lax.psum_scatter(lax.dot_general(pre_grad, up_weight, (((1,), (1,)), ((),...]
    gather x8 -> x0, local copies, waits for them, and re-layouts: 17.7 us -> none  [the longest x2 4.39 us: on_device(): neighbours = bank[row_part]]
    psum x1 -> x0, blocking collectives: 14.6 us -> none  [on_device(): lax.psum(partial_emb.astype(jnp.bfloat16), 'head').astype(jnp.float32)]
    unnamed x15 -> x20, local copies, waits for them, and re-layouts: 0.05 us -> 9.71 us
  transfers between devices with their start and end apart: 7 -> 0, of which waited for: 7 -> 0; matrix products, arithmetic and copies ran while one was open for 3% -> 0% of each run, Pallas kernels for 0% -> 0%
where the time goes in v2:
time: 126 us; the launch traced here: 125 us
  Pallas kernels  114 us (90%)
  local copies, waits for them, and re-layouts  10.4 us (8%)
    pallas_call x1, Pallas kernels, on_device(): pl.pallas_call(functools.partial(kernel, dims), out_shape=(jax.ShapeDtype...  114 us
    unnamed x20, local copies, waits for them, and re-layouts  9.71 us

profile of v2, /device:TPU:1, one launch (start us, length us, event | category | flops | bytes accessed | tf_op | source)
XLA Modules:
  0.0 124.9 jit_solution(6988311796503311806)
XLA Ops:
  0.6 0.7 reshape.11.bias_hbm
  1.3 0.0 copy-start
  1.3 1.3 %copy-done = bf16[768,768]{1,0:T(8,128)(2,1)S(1)} copy-done((bf16[768,768]{1,0:T(8,128)(2,1)S(1)}, bf16[768,768]{1,0:T(8,128)(2,1)}, u32[]{:S(2)}) %copy-start) | copy-done | bytes 1179672
  2.6 0.0 copy-start.1
  2.6 1.3 %copy-done.1 = bf16[768,768]{1,0:T(8,128)(2,1)S(1)} copy-done((bf16[768,768]{1,0:T(8,128)(2,1)S(1)}, bf16[768,768]{1,0:T(8,128)(2,1)}, u32[]{:S(2)}) %copy-start.1) | copy-done | bytes 1179672
  3.9 0.0 copy-start.2
  3.9 1.1 copy-done.2
  5.0 0.0 copy-start.3
  5.0 0.8 copy-done.3
  5.8 0.0 copy-start.4
  5.8 0.8 copy-done.4
  6.6 0.0 copy-start.5
  6.6 0.7 copy-done.5
  7.3 0.0 copy-start.6
  7.3 0.7 copy-done.6
  8.0 0.0 copy-start.7
  8.0 0.7 copy-done.7
  8.7 0.0 copy-start.8
  8.7 0.7 copy-done.8
  9.4 113.9 %shard_map.113 = (bf16[8,768]{1,0:T(8,128)(2,1)S(1)}, bf16[768,768]{1,0:T(8,128)(2,1)S(1)}) custom-call(bf16[32,768]{1,0:T(8,128)(2,1)S(1)} %copy-done.3, bf16[32,768]{1,0:T(8,128)(2,1)S(1)} %copy-done.4, s32[32,32]{1,0:T(8,128)S(1)} %copy-done.5, s32[32,32]{1,0:T(8,128)S(1)} %copy-done.6, f32[32,32]{1,0:T(8,128)S(1)} %copy-done.7, s32[1,512]{1,0:T(1,128)S(1)} %bitcast.1, ...), custom_call_target="tpu_custom_call" | custom-call | flops 4000000000 | bytes 6000000 | tf_op jit(solution)/shard_map/pallas_call | solution.py:530
  123.3 0.6 copy.14
  123.9 1.0 copy.15
Async XLA Ops:
  1.3 1.3 %copy-start = (bf16[768,768]{1,0:T(8,128)(2,1)S(1)}, bf16[768,768]{1,0:T(8,128)(2,1)}, u32[]{:S(2)}) copy-start(bf16[768,768]{1,0:T(8,128)(2,1)} %up_hbm.1) | copy-start | bytes 3538948
  2.6 1.3 %copy-start.1 = (bf16[768,768]{1,0:T(8,128)(2,1)S(1)}, bf16[768,768]{1,0:T(8,128)(2,1)}, u32[]{:S(2)}) copy-start(bf16[768,768]{1,0:T(8,128)(2,1)} %down_hbm.1) | copy-start | bytes 3538948
  3.9 1.1 copy-start.2
  5.0 0.8 copy-start.3
  5.8 0.8 copy-start.4
  6.6 0.7 copy-start.5
  7.3 0.7 copy-start.6
  8.0 0.7 copy-start.7
  8.7 0.7 copy-start.8

commit v3 on v2

--- a/solution.py
+++ b/solution.py
@@ -42,7 +42,7 @@
     in_hbm, pos_hbm, nb_hbm, nr_hbm, mg_hbm, home_hbm, bank_hbm, up_hbm, bias_hbm, down_hbm,
     gi_ref, gd_ref,
     in_ref, pos_ref, nb_ref, nr_ref, mg_ref, home_ref, bank_ref, up_ref, bias_ref, down_ref,
-    meta_all, e_all, ps_all, h_all, f_all, gd_all,
+    meta_all, e_all, ps_all, h_two, ht_send, ht_all, f_all, gd_all,
     xs, xr, xs2, xr2, xg, in_l, pos_l, dgelu,
     pm_sc, near_sc, q_sc, m_sc,
     g_own, g_send, gc_recv, gy_send, gy_recv, gz_send, gz_recv,
@@ -117,8 +117,8 @@
         return copy(src, dst, xsem, k * nx + d, xdev(d))
 
     pairs = [
+        (in_hbm, in_ref), (up_hbm, up_ref), (bias_hbm, bias_ref), (down_hbm, down_ref),
         (nb_hbm, nb_ref), (nr_hbm, nr_ref), (mg_hbm, mg_ref), (home_hbm, home_ref),
-        (in_hbm, in_ref), (up_hbm, up_ref), (bias_hbm, bias_ref), (down_hbm, down_ref),
         (pos_hbm, pos_ref), (bank_hbm, bank_ref),
     ]
     loads = [pltpu.make_async_copy(src, dst, lsem.at[i]) for i, (src, dst) in enumerate(pairs)]
@@ -127,11 +127,23 @@
 
     barrier = pltpu.get_barrier_semaphore()
     greet = [xcdev(d) for d in range(nx)] + [xdev(d) for d in range(1, nx)]
-    greet += [ydev(d) for d in range(1, ny)] + [zdev(o) for o in offs[1:]]
+    greet += [ydev(d) for d in range(1, ny)] + []
+    greet = [zdev(o) for o in offs[:0:-1]] + greet
     for dev in greet:
         pl.semaphore_signal(barrier, inc=1, device_id=dev, device_id_type=MESH)
 
     for cp in loads[:4]:
+        cp.wait()
+    queries = in_ref[...]
+    pre = dot(queries, up_ref[...]) + bias_ref[...].reshape(1, units)
+    t = jnp.tanh(K0 * (pre + K1 * (pre * pre * pre)))
+    hid = (0.5 * pre * (1.0 + t)).astype(BF16)
+    h_two[0] = hid
+    partial = dot(hid, down_ref[...])
+    for i in range(nx):
+        xs[i] = fold(partial[QH * i:QH * (i + 1)]).astype(BF16)
+
+    for cp in loads[4:8]:
         cp.wait()
     mine8 = pl.ds(pl.multiple_of(x * QH, QH), QH)
     lanes = 128 // NEG
@@ -160,22 +172,11 @@
     def zgather(k, s, ref):
         return zcopy(k, s, -offs[s], ref.at[0, pl.ds(0, 1)], ref.at[s // per, pl.ds(s % per, 1)])
 
+    for d in range(1, nx):
+        start(xcopy(0, d, xs.at[lax.rem(x + d, nx)], xr.at[d]))
     for s in far_first:
         start(zgather(0, s, meta_all))
-
-    for cp in loads[4:8]:
-        cp.wait()
-    queries = in_ref[...]
-    pre = dot(queries, up_ref[...]) + bias_ref[...]
-    t = jnp.tanh(K0 * (pre + K1 * (pre * pre * pre)))
-    hid = (0.5 * pre * (1.0 + t)).astype(BF16)
-    h_all[0, 0] = hid
-    partial = dot(hid, down_ref[...])
-    for i in range(nx):
-        xs[i] = fold(partial[QH * i:QH * (i + 1)]).astype(BF16)
-    for d in range(1, nx):
-        start(xcopy(0, d, xs.at[lax.rem(x + d, nx)], xr.at[d]))
-    start(ccopy(0, h_all.at[0, 0], h_all.at[0, 1]))
+    start(ccopy(0, h_two.at[0], h_two.at[1]))
     dgelu[...] = 0.5 * (1.0 + t) + 0.5 * pre * (1.0 - t * t) * (K0 * (1.0 + 3.0 * K1 * (pre * pre)))
     inf = queries.astype(F32)
     loads[8].wait()
@@ -219,6 +220,13 @@
     def emb_core(i, ref, k):
         return ccopy(i, ref.at[k, pl.ds(0, rings)], ref.at[k, pl.ds(rings, rings)])
 
+    ccopy(0, h_two.at[0], h_two.at[1]).wait_recv()
+    turned = jnp.concatenate([h_two[0].astype(F32), h_two[1].astype(F32)], axis=0).T
+    ht_send[...] = turned.astype(BF16).reshape(ht_send.shape)
+    for d in range(1, ny):
+        start(ycopy(0, d, ht_send.at[lax.rem(y + d, ny)], ht_all.at[ny - d]))
+    ht_all[0] = ht_send[y]
+
     for s in range(1, nz):
         zgather(0, s, meta_all).wait_recv()
 
@@ -229,7 +237,6 @@
 
     for d in range(1, ny):
         start(meta_y(d))
-    ccopy(0, h_all.at[0, 0], h_all.at[0, 1]).wait_recv()
     for d in range(1, ny):
         meta_y(d).wait_recv()
     meta_c = ccopy(1, meta_all.at[:, pl.ds(0, rings)], meta_all.at[:, pl.ds(rings, rings)])
@@ -240,7 +247,7 @@
 
     tri = jnp.where(iota((PAIRS, PAIRS), 0) <= iota((PAIRS, PAIRS), 1), 1.0, 0.0).astype(BF16)
     q_lane = (iota((block, PAIRS), 1) // NEG + 1).astype(F32)
-    for k in range(chunks):
+    def find(k):
         ids = meta_all[k, :, 0, pl.ds(0, PAIRS)].astype(I32)
         margins = meta_all[k, :, 0, pl.ds(PAIRS, PAIRS)]
         owner = ids // rows_own
@@ -332,20 +339,13 @@
             start(zcopy(3, s, offs[s], gz_send.at[k, s % per], gz_recv.at[s]))
             start(zcopy(4, s, offs[s], rz_send.at[k, s % per], rz_recv.at[s]))
 
-    def hidden_y():
-        for d in range(1, ny):
-            start(ycopy(0, d, h_all.at[0], h_all.at[ny - d]))
-
-    stages = [emb_z, emb_y, score, sum_core, sum_y]
-    lag = [0, 1, 2, 3, 4]
-    for step in range(1, chunks + len(stages) - 1):
+    find(0)
+    stages = [emb_z, find, emb_y, score, sum_core, sum_y]
+    lag = [0, 0, 1, 2, 3, 4]
+    for step in range(1, chunks + max(lag)):
         for stage, late in zip(stages, lag):
             if 0 <= step - late < chunks:
                 stage(step - late)
-        if step == chunks:
-            hidden_y()
-    if chunks + len(stages) - 2 < chunks:
-        hidden_y()
 
     wsum = g_own[0, 0]
     rsum = rz_send[0, 0]
@@ -380,6 +380,17 @@
     for d in range(1, ny):
         start(ycopy(18, d, f_all.at[0], f_all.at[ny - d]))
 
+    down_sum = dot(ht_all[0], f_all[0].reshape(nc * nx * QH, half))
+    for d in range(1, ny):
+        ycopy(0, d, ht_send.at[0], ht_all.at[ny - d]).wait_recv()
+        ycopy(18, d, f_all.at[0], f_all.at[ny - d]).wait_recv()
+        down_sum = down_sum + dot(ht_all[ny - d], f_all[ny - d].reshape(nc * nx * QH, half))
+    p_sc[...] = down_sum.astype(BF16).reshape(gd_pieces, 16, half)
+    for s in far_first:
+        zz = zat(offs[s])
+        piece = p_sc.at[jnp.minimum(zz, gd_pieces - 1)]
+        start(zcopy(5, s, offs[s], piece, pz_recv.at[s]), zz < gd_pieces)
+
     grad_all = jnp.concatenate([top, low], axis=1).astype(BF16)
     hidden_grad = dot(grad_all, down_ref[...], 1, 1)
     pre_grad = (hidden_grad * dgelu[...]).astype(BF16)
@@ -389,39 +400,28 @@
     for d in range(1, nx):
         start(xcopy(2, d, xs2.at[lax.rem(x + d, nx)], xr2.at[d]))
 
-    for d in range(1, ny):
-        ycopy(0, d, h_all.at[0], h_all.at[ny - d]).wait_recv()
-        ycopy(18, d, f_all.at[0], f_all.at[ny - d]).wait_recv()
-    count = ny * nc * nx * QH
-    down_sum = dot(h_all[...].reshape(count, units), f_all[...].reshape(count, half), 0, 0)
-    p_sc[...] = down_sum.astype(BF16).reshape(ny * gd_pieces, 16, half)
+    busy = z < gd_pieces
+    scale = 1.0 / math.sqrt(nx * QH * ny * nz * nc)
+
+    @pl.when(busy)
+    def _():
+        acc = p_sc[jnp.minimum(z, gd_pieces - 1)].astype(F32)
+        for s in range(1, nz):
+            zcopy(5, s, offs[s], p_sc.at[0], pz_recv.at[s]).wait_recv()
+            acc = acc + pz_recv[s].astype(F32)
+        gd_all[0, 0] = (acc * scale).astype(BF16)
+
+    def zlast(s):
+        return zgather(6, s, gd_all)
+
     for s in far_first:
-        zz = zat(offs[s])
-        piece = p_sc.at[y * gd_pieces + jnp.minimum(zz, gd_pieces - 1)]
-        start(zcopy(5, s, offs[s], piece, pz_recv.at[s]), zz < gd_pieces)
+        start(zlast(s), busy)
 
     carry = xs2[x].astype(F32) + gradient
     for d in range(1, nx):
         xcopy(2, d, xs2.at[0], xr2.at[d]).wait_recv()
         carry = carry + xr2[d].astype(F32)
     gi_ref[...] = unfold(carry).astype(BF16)
-
-    busy = z < gd_pieces
-    scale = 1.0 / math.sqrt(nx * QH * ny * nz * nc)
-
-    @pl.when(busy)
-    def _():
-        acc = p_sc[y * gd_pieces + jnp.minimum(z, gd_pieces - 1)].astype(F32)
-        for s in range(1, nz):
-            zcopy(5, s, offs[s], p_sc.at[0], pz_recv.at[s]).wait_recv()
-            acc = acc + pz_recv[s].astype(F32)
-        gd_all[0, 0] = (acc * scale).astype(BF16)
-
-    def zlast(s):
-        return zgather(6, s, gd_all)
-
-    for s in far_first:
-        start(zlast(s), busy)
 
     def last_z(k):
         for s in range(max(1, k * per), (k + 1) * per):
@@ -483,13 +483,15 @@
     V = pltpu.VMEM
     args = (
         inputs, positives, neg_block, neg_row, margins, block_home.reshape(1, -1), bank,
-        up_weight, up_bias.reshape(1, -1), down_weight,
+        up_weight, up_bias, down_weight,
     )
     scratch = [V(a.shape, a.dtype) for a in args] + [
         V((chunks, block, 1, 2 * PAIRS), F32),
         V((chunks, block, 16, half), BF16),
         V((chunks, block, 1, 128), F32),
-        V((ny, nc, queries, units), BF16),
+        V((nc, queries, units), BF16),
+        V((ny, units // ny, nc * queries), BF16),
+        V((ny, units // ny, nc * queries), BF16),
         V((ny, nc, queries, half), BF16),
         V((chunks, block, 16, half), BF16),
         V((nx, 16, half), BF16),
@@ -518,7 +520,7 @@
         V((chunks, ny, per, 1, 128), F32),
         V((chunks, per, 1, 128), F32),
         V((nz, 1, 128), F32),
-        V((ny * gd_pieces, 16, half), BF16),
+        V((gd_pieces, 16, half), BF16),
         V((nz, 16, half), BF16),
         pltpu.SemaphoreType.DMA((len(args),)),
         pltpu.SemaphoreType.DMA((2, 4 * nx)),
@@ -537,7 +539,7 @@
         out_specs=(vmem, vmem),
         scratch_shapes=scratch,
         compiler_params=pltpu.CompilerParams(
-            collective_id=0, has_side_effects=True, vmem_limit_bytes=40 * 1024 * 1024
+            collective_id=0, has_side_effects=True, vmem_limit_bytes=60 * 1024 * 1024
         ),
         cost_estimate=pl.CostEstimate(
             flops=4_000_000_000, bytes_accessed=6_000_000, transcendentals=30_000

time: 126 us -> 115 us (0.913)
  local copies, waits for them, and re-layouts: 10.4 us -> 3.67 us
  Pallas kernels: 114 us -> 111 us
    unnamed x20 -> x2, local copies, waits for them, and re-layouts: 9.71 us -> 3.67 us
    pallas_call x1, Pallas kernels: 114 us -> 111 us  [on_device(): pl.pallas_call(functools.partial(kernel, dims), out_shape=(jax.ShapeDtype...]
where the time goes in v3:
time: 115 us
  Pallas kernels  111 us (97%)
  local copies, waits for them, and re-layouts  3.67 us (3%)
    pallas_call x1, Pallas kernels, on_device(): pl.pallas_call(functools.partial(kernel, dims), out_shape=(jax.ShapeDtype...  111 us
    unnamed x2, local copies, waits for them, and re-layouts  3.67 us

profile of v3, /device:TPU:1, one launch (start us, length us, event | category | flops | bytes accessed | tf_op | source)
XLA Modules:
  0.0 115.1 jit_solution(1575747544055800591)
XLA Ops:
  0.6 110.8 %shard_map.113 = (bf16[8,768]{1,0:T(8,128)(2,1)}, bf16[768,768]{1,0:T(8,128)(2,1)}) custom-call(bf16[32,768]{1,0:T(8,128)(2,1)} %in_hbm.1, bf16[32,768]{1,0:T(8,128)(2,1)} %pos_hbm.1, s32[32,32]{1,0:T(8,128)} %nb_hbm.1, s32[32,32]{1,0:T(8,128)} %nr_hbm.1, f32[32,32]{1,0:T(8,128)} %mg_hbm.1, s32[1,512]{1,0:T(1,128)} %bitcast.1, bf16[512,768]{1,0:T(8,128)(2,1)} %bank_hbm.1, ...), custom_call_target="tpu_custom_call" | custom-call | flops 4000000000 | bytes 6000000 | tf_op jit(solution)/shard_map/pallas_call | solution.py:532
  111.5 1.3 %copy.14 = bf16[8,768]{1,0:T(8,128)(2,1)} copy(bf16[8,768]{1,0:T(8,128)(2,1)} %get-tuple-element.4) | data formatting | bytes 24576
  112.8 2.4 %copy.15 = bf16[768,768]{1,0:T(8,128)(2,1)} copy(bf16[768,768]{1,0:T(8,128)(2,1)} %get-tuple-element.5) | data formatting | bytes 2359296

commit v4 on v3

--- a/solution.py
+++ b/solution.py
@@ -88,6 +88,12 @@
     def ydev(d):
         return (bid(lax.rem(y + d, ny), z, c), x)
 
+    def piece_of(zz):
+        return zz * gd_pieces // nz
+
+    def owns(zz):
+        return piece_of(zz + 1) > piece_of(zz)
+
     cdev = xcdev(0)
     unsent = []
 
@@ -195,7 +201,7 @@
     s8 = s16[:QH] + s16[QH:]
     diag = iota((QH, 128), 0) == iota((QH, 128), 1)
     ps_all[0, 0] = jnp.sum(jnp.where(diag, s8, 0.0), axis=0, keepdims=True)
-    for s in far_first:
+    for s in range(1, nz):
         start(zgather(1, s, e_all))
         start(zgather(2, s, ps_all))
 
@@ -388,8 +394,7 @@
     p_sc[...] = down_sum.astype(BF16).reshape(gd_pieces, 16, half)
     for s in far_first:
         zz = zat(offs[s])
-        piece = p_sc.at[jnp.minimum(zz, gd_pieces - 1)]
-        start(zcopy(5, s, offs[s], piece, pz_recv.at[s]), zz < gd_pieces)
+        start(zcopy(5, s, offs[s], p_sc.at[piece_of(zz)], pz_recv.at[s]), owns(zz))
 
     grad_all = jnp.concatenate([top, low], axis=1).astype(BF16)
     hidden_grad = dot(grad_all, down_ref[...], 1, 1)
@@ -400,12 +405,12 @@
     for d in range(1, nx):
         start(xcopy(2, d, xs2.at[lax.rem(x + d, nx)], xr2.at[d]))
 
-    busy = z < gd_pieces
+    busy = owns(z)
     scale = 1.0 / math.sqrt(nx * QH * ny * nz * nc)
 
     @pl.when(busy)
     def _():
-        acc = p_sc[jnp.minimum(z, gd_pieces - 1)].astype(F32)
+        acc = p_sc[piece_of(z)].astype(F32)
         for s in range(1, nz):
             zcopy(5, s, offs[s], p_sc.at[0], pz_recv.at[s]).wait_recv()
             acc = acc + pz_recv[s].astype(F32)
@@ -425,7 +430,7 @@
 
     def last_z(k):
         for s in range(max(1, k * per), (k + 1) * per):
-            pl.when(zat(offs[s]) < gd_pieces)(zlast(s).wait_recv)
+            pl.when(owns(zat(offs[s])))(zlast(s).wait_recv)
         for d in range(1, ny):
             start(ycopy(19 + k, d, near_ring(gd_all, k), near_ring(gd_all, k, ny - d)))
 
@@ -440,11 +445,11 @@
         for s in range(per):
             zz = zat(offs[k * per + s])
 
-            @pl.when(zz < gd_pieces)
+            @pl.when(owns(zz))
             def _():
                 for d in range(ny):
                     yy = lax.rem(y + d, ny)
-                    row = pl.multiple_of((yy * gd_pieces + zz) * 16, 16)
+                    row = pl.multiple_of((yy * gd_pieces + piece_of(zz)) * 16, 16)
                     col = pl.multiple_of(at * half, 128)
                     gd_ref[pl.ds(row, 16), pl.ds(col, half)] = gd_all[k, cr * rings + d * per + s]
 
@@ -532,8 +537,8 @@
     return pl.pallas_call(
         functools.partial(kernel, dims),
         out_shape=(
-            jax.ShapeDtypeStruct((QH, width), BF16),
-            jax.ShapeDtypeStruct((units, width), BF16),
+            pltpu.VMEM((QH, width), BF16),
+            pltpu.VMEM((units, width), BF16),
         ),
         in_specs=[pl.BlockSpec(memory_space=pltpu.HBM)] * len(args),
         out_specs=(vmem, vmem),

time: 115 us -> 109 us (0.948)
  Pallas kernels: 111 us -> 106 us
  local copies, waits for them, and re-layouts: 3.67 us -> 1.61 us
    pallas_call x1, Pallas kernels: 111 us -> 106 us  [on_device(): pl.pallas_call(functools.partial(kernel, dims), out_shape=(pltpu.VMEM((QH...]
    unnamed x2, local copies, waits for them, and re-layouts: 3.67 us -> 1.61 us
where the time goes in v4:
time: 109 us
  Pallas kernels  106 us (97%)
  local copies, waits for them, and re-layouts  1.61 us (1%)
    pallas_call x1, Pallas kernels, on_device(): pl.pallas_call(functools.partial(kernel, dims), out_shape=(pltpu.VMEM((QH...  106 us

profile of v4, /device:TPU:1, one launch (start us, length us, event | category | flops | bytes accessed | tf_op | source)
XLA Modules:
  0.0 108.7 jit_solution(4442792708945252107)
XLA Ops:
  0.6 106.4 %shard_map.113 = (bf16[8,768]{1,0:T(8,128)(2,1)S(1)}, bf16[768,768]{1,0:T(8,128)(2,1)S(1)}) custom-call(bf16[32,768]{1,0:T(8,128)(2,1)} %in_hbm.1, bf16[32,768]{1,0:T(8,128)(2,1)} %pos_hbm.1, s32[32,32]{1,0:T(8,128)} %nb_hbm.1, s32[32,32]{1,0:T(8,128)} %nr_hbm.1, f32[32,32]{1,0:T(8,128)} %mg_hbm.1, s32[1,512]{1,0:T(1,128)} %bitcast.1, ...), custom_call_target="tpu_custom_call" | custom-call | flops 4000000000 | bytes 6000000 | tf_op jit(solution)/shard_map/pallas_call | solution.py:537
  107.1 0.6 copy.14
  107.7 1.0 copy.15

commit v5 on v4

--- a/solution.py
+++ b/solution.py
@@ -94,6 +94,8 @@
     def owns(zz):
         return piece_of(zz + 1) > piece_of(zz)
 
+    ys = sorted(range(1, ny), key=lambda d: -min(d, ny - d))
+    xsd = sorted(range(1, nx), key=lambda d: -min(d, nx - d))
     cdev = xcdev(0)
     unsent = []
 
@@ -178,7 +180,7 @@
     def zgather(k, s, ref):
         return zcopy(k, s, -offs[s], ref.at[0, pl.ds(0, 1)], ref.at[s // per, pl.ds(s % per, 1)])
 
-    for d in range(1, nx):
+    for d in xsd:
         start(xcopy(0, d, xs.at[lax.rem(x + d, nx)], xr.at[d]))
     for s in far_first:
         start(zgather(0, s, meta_all))
@@ -212,7 +214,7 @@
         for s in range(max(1, k * per), (k + 1) * per):
             zgather(1, s, e_all).wait_recv()
             zgather(2, s, ps_all).wait_recv()
-        for d in range(1, ny):
+        for d in ys:
             start(ycopy(2 + k, d, near_ring(e_all, k), near_ring(e_all, k, ny - d)))
             start(ycopy(6 + k, d, near_ring(ps_all, k), near_ring(ps_all, k, ny - d)))
 
@@ -229,7 +231,7 @@
     ccopy(0, h_two.at[0], h_two.at[1]).wait_recv()
     turned = jnp.concatenate([h_two[0].astype(F32), h_two[1].astype(F32)], axis=0).T
     ht_send[...] = turned.astype(BF16).reshape(ht_send.shape)
-    for d in range(1, ny):
+    for d in ys:
         start(ycopy(0, d, ht_send.at[lax.rem(y + d, ny)], ht_all.at[ny - d]))
     ht_all[0] = ht_send[y]
 
@@ -241,7 +243,7 @@
             1, d, meta_all.at[:, pl.ds(0, per)], meta_all.at[:, pl.ds((ny - d) * per, per)]
         )
 
-    for d in range(1, ny):
+    for d in ys:
         start(meta_y(d))
     for d in range(1, ny):
         meta_y(d).wait_recv()
@@ -316,7 +318,7 @@
     def sum_core(k):
         ccopy(10 + k, g_send.at[k], gc_recv.at[k]).wait_recv()
         ccopy(14 + k, r_send.at[k], rc_recv.at[k]).wait_recv()
-        for d in list(range(1, ny)) + [0]:
+        for d in ys + [0]:
             at = pl.ds(d * per, per)
             g_sum = g_own[k, at] + gc_recv[k, at].astype(F32)
             r_sum = r_own[k, at] + rc_recv[k, at]
@@ -345,13 +347,17 @@
             start(zcopy(3, s, offs[s], gz_send.at[k, s % per], gz_recv.at[s]))
             start(zcopy(4, s, offs[s], rz_send.at[k, s % per], rz_recv.at[s]))
 
-    find(0)
-    stages = [emb_z, find, emb_y, score, sum_core, sum_y]
-    lag = [0, 0, 1, 2, 3, 4]
-    for step in range(1, chunks + max(lag)):
-        for stage, late in zip(stages, lag):
-            if 0 <= step - late < chunks:
-                stage(step - late)
+    if chunks == 4:
+        order = [
+            ("f", 0), ("f", 1), ("z", 1), ("y", 0), ("f", 2), ("z", 2), ("y", 1), ("s", 0),
+            ("f", 3), ("s", 1), ("c", 0), ("z", 3), ("y", 2), ("c", 1), ("s", 2), ("a", 0),
+            ("y", 3), ("c", 2), ("a", 1), ("s", 3), ("a", 2), ("c", 3), ("a", 3),
+        ]
+    else:
+        order = [(name, k) for name in "fzysca" for k in range(chunks) if name + str(k) != "z0"]
+    does = {"f": find, "z": emb_z, "y": emb_y, "s": score, "c": sum_core, "a": sum_y}
+    for name, k in order:
+        does[name](k)
 
     wsum = g_own[0, 0]
     rsum = rz_send[0, 0]
@@ -364,7 +370,7 @@
     rcol = jnp.sum(jnp.where(lane_q, rsum, 0.0), axis=1, keepdims=True)
     gradient = 2.0 * pos_l[x] * rcol - 2.0 * wsum
     xg[0, x] = gradient.astype(BF16)
-    for d in range(1, nx):
+    for d in xsd:
         start(xcopy(1, d, xg.at[0, x], xg.at[0, x]))
     for d in range(nx):
         start(copy(xg.at[0, x], xg.at[1, x], xsem, 3 * nx + d, xcdev(d)))
@@ -383,7 +389,7 @@
 
     top, low = halves(0)
     halves(1)
-    for d in range(1, ny):
+    for d in ys:
         start(ycopy(18, d, f_all.at[0], f_all.at[ny - d]))
 
     down_sum = dot(ht_all[0], f_all[0].reshape(nc * nx * QH, half))
@@ -402,7 +408,7 @@
     carried = dot(pre_grad, up_ref[...], 1, 1)
     for i in range(nx):
         xs2[i] = fold(carried[QH * i:QH * (i + 1)]).astype(BF16)
-    for d in range(1, nx):
+    for d in xsd:
         start(xcopy(2, d, xs2.at[lax.rem(x + d, nx)], xr2.at[d]))
 
     busy = owns(z)
@@ -419,7 +425,7 @@
     def zlast(s):
         return zgather(6, s, gd_all)
 
-    for s in far_first:
+    for s in range(1, nz):
         start(zlast(s), busy)
 
     carry = xs2[x].astype(F32) + gradient
@@ -431,7 +437,7 @@
     def last_z(k):
         for s in range(max(1, k * per), (k + 1) * per):
             pl.when(owns(zat(offs[s])))(zlast(s).wait_recv)
-        for d in range(1, ny):
+        for d in ys:
             start(ycopy(19 + k, d, near_ring(gd_all, k), near_ring(gd_all, k, ny - d)))
 
     def last_y(k):

time: 109 us -> 107 us (0.982)
  Pallas kernels: 106 us -> 104 us
    pallas_call x1, Pallas kernels: 106 us -> 104 us  [on_device(): pl.pallas_call(functools.partial(kernel, dims), out_shape=(pltpu.VMEM((QH...]
where the time goes in v5:
time: 107 us
  Pallas kernels  104 us (97%)
  local copies, waits for them, and re-layouts  1.61 us (2%)
    pallas_call x1, Pallas kernels, on_device(): pl.pallas_call(functools.partial(kernel, dims), out_shape=(pltpu.VMEM((QH...  104 us

profile of v5, /device:TPU:1, one launch (start us, length us, event | category | flops | bytes accessed | tf_op | source)
XLA Modules:
  0.0 106.7 jit_solution(7412593938810515546)
XLA Ops:
  0.6 104.5 %shard_map.113 = (bf16[8,768]{1,0:T(8,128)(2,1)S(1)}, bf16[768,768]{1,0:T(8,128)(2,1)S(1)}) custom-call(bf16[32,768]{1,0:T(8,128)(2,1)} %in_hbm.1, bf16[32,768]{1,0:T(8,128)(2,1)} %pos_hbm.1, s32[32,32]{1,0:T(8,128)} %nb_hbm.1, s32[32,32]{1,0:T(8,128)} %nr_hbm.1, f32[32,32]{1,0:T(8,128)} %mg_hbm.1, s32[1,512]{1,0:T(1,128)} %bitcast.1, ...), custom_call_target="tpu_custom_call" | custom-call | flops 4000000000 | bytes 6000000 | tf_op jit(solution)/shard_map/pallas_call | solution.py:543
  105.1 0.6 copy.14
  105.7 1.0 copy.15

commit v6 on v5

--- a/solution.py
+++ b/solution.py
@@ -112,6 +112,14 @@
             pl.when(when)(cp.start)
         unsent.append((cp, when))
 
+    def drain(count):
+        for cp, when in unsent[:count]:
+            if when is None:
+                cp.wait_send()
+            else:
+                pl.when(when)(cp.wait_send)
+        del unsent[:count]
+
     def zcopy(k, s, off, src, dst):
         return copy(src, dst, zsem, k * nz + s, zdev(off))
 
@@ -227,13 +235,6 @@
 
     def emb_core(i, ref, k):
         return ccopy(i, ref.at[k, pl.ds(0, rings)], ref.at[k, pl.ds(rings, rings)])
-
-    ccopy(0, h_two.at[0], h_two.at[1]).wait_recv()
-    turned = jnp.concatenate([h_two[0].astype(F32), h_two[1].astype(F32)], axis=0).T
-    ht_send[...] = turned.astype(BF16).reshape(ht_send.shape)
-    for d in ys:
-        start(ycopy(0, d, ht_send.at[lax.rem(y + d, ny)], ht_all.at[ny - d]))
-    ht_all[0] = ht_send[y]
 
     for s in range(1, nz):
         zgather(0, s, meta_all).wait_recv()
@@ -359,6 +360,13 @@
     for name, k in order:
         does[name](k)
 
+    ccopy(0, h_two.at[0], h_two.at[1]).wait_recv()
+    turned = jnp.concatenate([h_two[0].astype(F32), h_two[1].astype(F32)], axis=0).T
+    ht_send[...] = turned.astype(BF16).reshape(ht_send.shape)
+    for d in ys:
+        start(ycopy(0, d, ht_send.at[lax.rem(y + d, ny)], ht_all.at[ny - d]))
+    ht_all[0] = ht_send[y]
+
     wsum = g_own[0, 0]
     rsum = rz_send[0, 0]
     for s in range(1, nz):
@@ -392,6 +400,7 @@
     for d in ys:
         start(ycopy(18, d, f_all.at[0], f_all.at[ny - d]))
 
+    older = len(unsent)
     down_sum = dot(ht_all[0], f_all[0].reshape(nc * nx * QH, half))
     for d in range(1, ny):
         ycopy(0, d, ht_send.at[0], ht_all.at[ny - d]).wait_recv()
@@ -411,6 +420,7 @@
     for d in xsd:
         start(xcopy(2, d, xs2.at[lax.rem(x + d, nx)], xr2.at[d]))
 
+    drain(older)
     busy = owns(z)
     scale = 1.0 / math.sqrt(nx * QH * ny * nz * nc)
 
@@ -469,11 +479,7 @@
             if 0 <= step - late < chunks:
                 stage(step - late)
 
-    for cp, when in unsent:
-        if when is None:
-            cp.wait_send()
-        else:
-            pl.when(when)(cp.wait_send)
+    drain(len(unsent))
 
 
 def on_device(

time: 107 us -> 106 us (level)
  no operation moved by 1% of the time
where the time goes in v6:
time: 106 us
  Pallas kernels  103 us (97%)
  local copies, waits for them, and re-layouts  1.61 us (2%)
    pallas_call x1, Pallas kernels, on_device(): pl.pallas_call(functools.partial(kernel, dims), out_shape=(pltpu.VMEM((QH...  103 us

profile of v6, /device:TPU:1, one launch (start us, length us, event | category | flops | bytes accessed | tf_op | source)
XLA Modules:
  0.0 105.8 jit_solution(16225413660773325428)
XLA Ops:
  0.6 103.5 %shard_map.113 = (bf16[8,768]{1,0:T(8,128)(2,1)S(1)}, bf16[768,768]{1,0:T(8,128)(2,1)S(1)}) custom-call(bf16[32,768]{1,0:T(8,128)(2,1)} %in_hbm.1, bf16[32,768]{1,0:T(8,128)(2,1)} %pos_hbm.1, s32[32,32]{1,0:T(8,128)} %nb_hbm.1, s32[32,32]{1,0:T(8,128)} %nr_hbm.1, f32[32,32]{1,0:T(8,128)} %mg_hbm.1, s32[1,512]{1,0:T(1,128)} %bitcast.1, ...), custom_call_target="tpu_custom_call" | custom-call | flops 4000000000 | bytes 6000000 | tf_op jit(solution)/shard_map/pallas_call | solution.py:549
  104.1 0.6 copy.14
  104.7 1.0 copy.15

commit v7 on v6

--- a/solution.py
+++ b/solution.py
@@ -213,6 +213,7 @@
     ps_all[0, 0] = jnp.sum(jnp.where(diag, s8, 0.0), axis=0, keepdims=True)
     for s in range(1, nz):
         start(zgather(1, s, e_all))
+    for s in range(1, nz):
         start(zgather(2, s, ps_all))
 
     def near_ring(ref, k, d=0):
@@ -437,6 +438,8 @@
 
     for s in range(1, nz):
         start(zlast(s), busy)
+
+    drain(len(unsent) - (nz - 1))
 
     carry = xs2[x].astype(F32) + gradient
     for d in range(1, nx):

time: 106 us -> 109 us (1.028)
  Pallas kernels: 103 us -> 106 us
    pallas_call x1, Pallas kernels: 103 us -> 106 us  [on_device(): pl.pallas_call(functools.partial(kernel, dims), out_shape=(pltpu.VMEM((QH...]
where the time goes in v7:
time: 109 us
  Pallas kernels  106 us (97%)
  local copies, waits for them, and re-layouts  1.61 us (1%)
    pallas_call x1, Pallas kernels, on_device(): pl.pallas_call(functools.partial(kernel, dims), out_shape=(pltpu.VMEM((QH...  106 us

profile of v7, /device:TPU:1, one launch (start us, length us, event | category | flops | bytes accessed | tf_op | source)
XLA Modules:
  0.0 108.7 jit_solution(12336930580102840514)
XLA Ops:
  0.6 106.5 %shard_map.113 = (bf16[8,768]{1,0:T(8,128)(2,1)S(1)}, bf16[768,768]{1,0:T(8,128)(2,1)S(1)}) custom-call(bf16[32,768]{1,0:T(8,128)(2,1)} %in_hbm.1, bf16[32,768]{1,0:T(8,128)(2,1)} %pos_hbm.1, s32[32,32]{1,0:T(8,128)} %nb_hbm.1, s32[32,32]{1,0:T(8,128)} %nr_hbm.1, f32[32,32]{1,0:T(8,128)} %mg_hbm.1, s32[1,512]{1,0:T(1,128)} %bitcast.1, ...), custom_call_target="tpu_custom_call" | custom-call | flops 4000000000 | bytes 6000000 | tf_op jit(solution)/shard_map/pallas_call | solution.py:552
  107.1 0.6 copy.14
  107.7 1.0 copy.15
